TPU v7x, 128 devices: a whole 4x4x4 slice. The times are simulated.
128 devices in a mesh: bx: 4 (over y_hi, core), by: 32 (over x, z, y_lo).
Axes of the slice: x: 4, y: 4 (y_hi: 2, y_lo: 2; y = y_hi * 2 + y_lo), z: 4, core: 2. Of those that a mesh axis runs over, the one named last changes fastest.
Arguments:
- features: bfloat16 [16384, 256], P(('bx', 'by')), may hold values from -6 to 6
- depth_logits: float32 [64, 16384], P(None, ('bx', 'by')), may hold values from -300 to 300
- ctx_weight: bfloat16 [256, 128], replicated, may hold values from -0.375 to 0.375
- point_pixel: int32 [524288], P(('bx', 'by')), may hold values from 0 to 127
- point_bin: int32 [524288], P(('bx', 'by')), may hold values from 0 to 63
- segment_count: int32 [128, 128], P(('bx', 'by')), may hold values from 0 to 64, as said below
- slot_cell: int32 [128, 128, 64], P(('bx', 'by')), may hold values from 0 to 8191
- conv_weight: bfloat16 [3, 3, 128, 128], replicated, may hold values from -0.1875 to 0.1875
- proj_weight: bfloat16 [128, 6], replicated, may hold values from -0.5 to 0.5
- level_count: int32 [6], replicated, may hold values from 3 to 8
- code_grad: float32 [6, 512, 2048], P(None, 'bx', 'by'), may hold values from -6 to 6
Outputs:
- fsq_codes: float32 [6, 512, 2048], P(None, 'bx', 'by')
- grad_logits: float32 [64, 16384], P(None, ('bx', 'by'))
- grad_features: bfloat16 [16384, 256], P(('bx', 'by'))
- grad_conv: float32 [3, 3, 128, 128], replicated
- grad_proj: float32 [128, 6], replicated
Inputs may be any that keep to these rules, and one draw needn't show every extreme that they name: `segment_count`: entry [s, d] is the number of device s's points bound for tile d; each row sums to 4096; some tile receives 64 points from every device. `slot_cell`: entry [d, s, j] is the row-major cell within tile d of the j-th point that device s sends to tile d; entries with j at or beyond segment_count[s, d] are unused.
All inputs are finite; a program needn't handle non-finite values.
Results may differ from a plain program's by a relative error of at most 0.011.
Values may be sent and summed in bfloat16 or wider, within the bound.
A program may use at most 128 MiB of HBM per device.

v0:
```python
import jax
import jax.numpy as jnp
from jax import lax
from jax.sharding import PartitionSpec as P

epsilon = 1e-05


def extended(block, sides, width):
    for axis, dim in sides:
        count = lax.axis_size(axis)
        forward = [(i, i + 1) for i in range(count - 1)]
        backward = [(target, source) for source, target in forward]
        low = lax.ppermute(
            lax.slice_in_dim(block, block.shape[dim] - width, None, axis=dim), axis, forward
        )
        high = lax.ppermute(lax.slice_in_dim(block, 0, width, axis=dim), axis, backward)
        block = jnp.concatenate([low, block, high], axis=dim)
    return block


def plane_dot(window, weight):
    rows, cols, depth = window.shape
    flat = jnp.dot(window.reshape(rows * cols, depth), weight, preferred_element_type=jnp.float32)
    return flat.reshape(rows, cols, weight.shape[1])


def conv_taps(padded, weight, tile_rows, tile_cols):
    summed = jnp.zeros((tile_rows, tile_cols, weight.shape[3]), jnp.float32)
    for row_tap in range(3):
        for col_tap in range(3):
            window = padded[row_tap : row_tap + tile_rows, col_tap : col_tap + tile_cols, :]
            summed = summed + plane_dot(window, weight[row_tap, col_tap])
    return summed


def conv_back(padded_grad, weight, tile_rows, tile_cols):
    summed = jnp.zeros((tile_rows, tile_cols, weight.shape[2]), jnp.float32)
    for row_tap in range(3):
        for col_tap in range(3):
            window = padded_grad[
                2 - row_tap : 2 - row_tap + tile_rows, 2 - col_tap : 2 - col_tap + tile_cols, :
            ]
            summed = summed + plane_dot(window, weight[row_tap, col_tap].T)
    return summed


def conv_weights_grad(padded, conv_grad, tile_rows, tile_cols):
    depth = padded.shape[2]
    grad_flat = conv_grad.reshape(tile_rows * tile_cols, conv_grad.shape[2])
    stacked = []
    for row_tap in range(3):
        line = []
        for col_tap in range(3):
            window = padded[
                row_tap : row_tap + tile_rows, col_tap : col_tap + tile_cols, :
            ].reshape(tile_rows * tile_cols, depth)
            line.append(
                lax.dot_general(
                    window, grad_flat, (((0,), (0,)), ((), ())), preferred_element_type=jnp.float32
                )
            )
        stacked.append(jnp.stack(line))
    return jnp.stack(stacked)


def encode_tile(padded, conv_weight, proj_weight, level_count, code_grad, tile_rows, tile_cols):
    conv_out = conv_taps(padded, conv_weight, tile_rows, tile_cols)
    inv_rms = lax.rsqrt(jnp.mean(conv_out * conv_out, axis=-1, keepdims=True) + epsilon)
    normed = conv_out * inv_rms
    hidden = jax.nn.silu(normed).astype(jnp.bfloat16)
    channels = hidden.shape[2]
    code_dims = proj_weight.shape[1]
    hidden_flat = hidden.reshape(tile_rows * tile_cols, channels)
    latent = jnp.dot(hidden_flat, proj_weight, preferred_element_type=jnp.float32).T.reshape(
        code_dims, tile_rows, tile_cols
    )
    half_levels = (level_count.astype(jnp.float32) - 1.0) * 0.5
    squash = jnp.tanh(latent)
    fsq_codes = half_levels[:, None, None] * squash
    code_slope = code_grad * half_levels[:, None, None] * (1.0 - squash * squash)
    slope_flat = code_slope.reshape(code_dims, tile_rows * tile_cols)
    proj_part = jnp.dot(
        hidden_flat.astype(jnp.float32).T, slope_flat.T, precision=lax.Precision.HIGHEST
    )
    hidden_grad = jnp.dot(
        slope_flat.T, proj_weight.astype(jnp.float32).T, precision=lax.Precision.HIGHEST
    ).reshape(tile_rows, tile_cols, channels)
    gate_sig = jax.nn.sigmoid(normed)
    norm_grad = hidden_grad * gate_sig * (1.0 + normed * (1.0 - gate_sig))
    mixed_term = jnp.mean(norm_grad * conv_out, axis=-1, keepdims=True)
    conv_grad = (inv_rms * norm_grad - conv_out * inv_rms * inv_rms * inv_rms * mixed_term).astype(
        jnp.bfloat16
    )
    return (fsq_codes, proj_part, conv_grad)


def slot_values(counts, pixel_list, depth_list, depth_prob, context, capacity):
    tile_count = counts.shape[0]
    pix_count = context.shape[0]
    starts = jnp.cumsum(counts) - counts
    slot_lane = jnp.arange(capacity, dtype=jnp.int32)
    slot_index = jnp.minimum(starts[:, None] + slot_lane[None, :], pixel_list.shape[0] - 1)
    usable = slot_lane[None, :] < counts[:, None]
    pixels = pixel_list[slot_index]
    depths = depth_list[slot_index]
    point_weight = jnp.where(usable, depth_prob[depths, pixels], 0.0)
    pixel_hot = pixels.reshape(-1)[:, None] == jnp.arange(pix_count, dtype=jnp.int32)[None, :]
    ctx_rows = jnp.dot(
        pixel_hot.astype(jnp.bfloat16), context, preferred_element_type=jnp.float32
    ).reshape(tile_count, capacity, -1)
    return (depths, usable, point_weight, ctx_rows, pixel_hot.astype(jnp.float32))


def slot_grads(
    back_grads, depths, usable, point_weight, ctx_rows, pixel_hot, depth_prob, ctx_weight
):
    bin_count = depth_prob.shape[0]
    channels = ctx_rows.shape[2]
    grads_f = back_grads.astype(jnp.float32)
    pair_dot = jnp.where(usable, jnp.sum(grads_f * ctx_rows, axis=-1), 0.0).reshape(-1)
    bin_hot = (
        depths.reshape(-1)[:, None] == jnp.arange(bin_count, dtype=jnp.int32)[None, :]
    ).astype(jnp.float32) * pair_dot[:, None]
    prob_grad = jnp.dot(bin_hot.T, pixel_hot, precision=lax.Precision.HIGHEST)
    weighted = (point_weight[..., None] * grads_f).reshape(-1, channels)
    ctx_grad = jnp.dot(pixel_hot.T, weighted, precision=lax.Precision.HIGHEST).astype(jnp.bfloat16)
    logit_grad = depth_prob * (prob_grad - jnp.sum(depth_prob * prob_grad, axis=0, keepdims=True))
    feature_grad = jnp.dot(ctx_grad, ctx_weight.T, preferred_element_type=jnp.float32).astype(
        jnp.bfloat16
    )
    return (logit_grad, feature_grad)


def framed(field):
    return extended(field, (("bx", 0), ("by", 1)), 1)


def per_device(
    features,
    depth_logits,
    ctx_weight,
    point_pixel,
    point_bin,
    segment_count,
    slot_cell,
    conv_weight,
    proj_weight,
    level_count,
    code_grad,
):
    grid_rows = lax.axis_size("bx")
    grid_cols = lax.axis_size("by")
    tile_count = grid_rows * grid_cols
    capacity = slot_cell.shape[2]
    tile_rows = code_grad.shape[1]
    tile_cols = code_grad.shape[2]
    channels = ctx_weight.shape[1]
    depth_prob = jax.nn.softmax(depth_logits, axis=0)
    context = jnp.dot(features, ctx_weight, preferred_element_type=jnp.float32).astype(jnp.bfloat16)
    depths, usable, point_weight, ctx_rows, pixel_hot = slot_values(
        segment_count[0], point_pixel, point_bin, depth_prob, context, capacity
    )
    carried = (point_weight[..., None] * ctx_rows).astype(jnp.bfloat16)
    arrived = lax.all_to_all(carried, ("bx", "by"), split_axis=0, concat_axis=0, tiled=True)
    targets = slot_cell[0].reshape(-1)
    pooled = jax.ops.segment_sum(
        arrived.reshape(-1, channels).astype(jnp.float32),
        targets,
        num_segments=tile_rows * tile_cols,
    )
    lifted = pooled.reshape(tile_rows, tile_cols, channels).astype(jnp.bfloat16)
    padded = framed(lifted)
    fsq_codes, proj_part, conv_grad = encode_tile(
        padded, conv_weight, proj_weight, level_count, code_grad, tile_rows, tile_cols
    )
    padded_grad = framed(conv_grad)
    lift_grad = (
        conv_back(padded_grad, conv_weight, tile_rows, tile_cols)
        .astype(jnp.bfloat16)
        .reshape(-1, channels)
    )
    conv_part = conv_weights_grad(padded, conv_grad, tile_rows, tile_cols)
    cell_grads = lift_grad[targets].reshape(tile_count, capacity, channels)
    back_grads = lax.all_to_all(cell_grads, ("bx", "by"), split_axis=0, concat_axis=0, tiled=True)
    grad_logits, grad_features = slot_grads(
        back_grads, depths, usable, point_weight, ctx_rows, pixel_hot, depth_prob, ctx_weight
    )
    grad_conv, grad_proj = lax.psum((conv_part, proj_part), ("bx", "by"))
    return (fsq_codes, grad_logits, grad_features, grad_conv, grad_proj)


def solution(mesh):
    return jax.shard_map(
        per_device,
        mesh=mesh,
        in_specs=(
            P(("bx", "by"), None),
            P(None, ("bx", "by")),
            P(),
            P(("bx", "by")),
            P(("bx", "by")),
            P(("bx", "by"), None),
            P(("bx", "by"), None, None),
            P(),
            P(),
            P(),
            P(None, "bx", "by"),
        ),
        out_specs=(P(None, "bx", "by"), P(None, ("bx", "by")), P(("bx", "by"), None), P(), P()),
        check_vma=False,
    )
```

profile of v0, /device:TPU:1, one launch (start us, length us, event | category | flops | bytes accessed | tf_op | source)
XLA Modules:
  0.0 586.6 jit_solution(510022887209339298)
XLA Ops:
  9.1 45.5 %gather_fusion.1 = s32[8192]{0:T(1024)S(1)} fusion(s32[4096]{0:T(1024)S(1)} %copy-done.1, s32[8192]{0:T(1024)S(1)} %broadcast_clamp_fusion.1), kind=kCustom, calls=%fused_computation.1 | custom fusion | bytes 98304 | tf_op jit(solution)/shard_map/gather | solution.py:105
  55.4 45.5 %gather_fusion = s32[8192]{0:T(1024)S(1)} fusion(s32[4096]{0:T(1024)S(1)} %copy-done.2, s32[8192]{0:T(1024)S(1)} %broadcast_clamp_fusion.1), kind=kCustom, calls=%fused_computation | custom fusion | bytes 98304 | tf_op jit(solution)/shard_map/gather | solution.py:106
  101.6 50.7 %gather_fusion.2 = f32[8192]{0:T(1024)S(1)} fusion(f32[64,128]{1,0:T(8,128)S(1)} %fusion.116, s32[8192]{0:T(1024)S(1)} %reshape.336), kind=kCustom, calls=%fused_computation.2 | custom fusion | bytes 131072 | tf_op jit(solution)/shard_map/gather | solution.py:107
  152.5 4.8 multiply_convert_fusion.1
  157.3 11.5 %all-to-all-start = ((bf16[128,64,128]{2,1,0:T(8,128)(2,1)}), bf16[128,64,128]{2,1,0:T(8,128)(2,1)S(1)}, u32[]{:S(2)}, u32[]{:S(2)}) async-start(bf16[128,64,128]{2,1,0:T(8,128)(2,1)} %get-tuple-element.36), calls=%async_computation | async-start | bytes 4194304 | tf_op jit(solution)/shard_map/all_to_all | solution.py:165
  170.4 28.8 %all-to-all-done = bf16[128,64,128]{2,1,0:T(8,128)(2,1)S(1)} async-done(((bf16[128,64,128]{2,1,0:T(8,128)(2,1)}), bf16[128,64,128]{2,1,0:T(8,128)(2,1)S(1)}, u32[]{:S(2)}, u32[]{:S(2)}) %all-to-all-start) | async-done | bytes 2097184 | tf_op jit(solution)/shard_map/all_to_all | solution.py:165
  199.2 46.4 %scatter_custom_fusion = f32[8192,128]{1,0:T(8,128)} fusion(s32[8192]{0:T(1024)S(1)} %reshape.352, bf16[8192,128]{1,0:T(8,128)(2,1)S(1)} %bitcast.158, f32[]{:T(128)} %constant.15.clone.1), kind=kCustom, calls=%fused_computation.10 | custom fusion | flops 2097152 | bytes 6291460 | tf_op jit(solution)/shard_map/scatter-add | solution.py:167
  245.7 2.4 convert_element_type.50
  248.2 3.3 collective-permute-start
  251.5 1.9 collective-permute-start.1
  253.5 4.4 fusion.106
  257.9 1.4 copy.83
  259.3 2.8 collective-permute-start.2
  262.2 1.5 collective-permute-start.3
  263.7 2.7 fusion.58
  266.3 2.7 fusion.60
  269.1 3.3 pad_maximum_fusion
  272.4 3.1 fusion.40
  275.4 2.7 fusion.48
  278.1 2.7 fusion.44
  280.9 2.7 fusion.52
  283.6 2.8 fusion.56
  286.3 13.3 %multiply_reduce_fusion.1 = (f32[128,64]{0,1:T(8,128)S(1)}, f32[128,64,128]{2,0,1:T(8,128)S(1)}) fusion(bf16[3,3,128,128]{3,2,1,0:T(8,128)(2,1)S(1)} %copy-done.18, bf16[130,65,128]{2,0,1:T(8,128)(2,1)} %copy-done.8, f32[128,64,128]{2,0,1:T(8,128)} %fusion.60, f32[128,64,128]{2,0,1:T(8,128)} %fusion.40, f32[128,64,128]{2,0,1:T(8,128)} %fusion.44, ...), kind=kOutput, calls=%fused_computation.18 | convolution fusion | flops 278913024 | bytes 39911424 | tf_op jit(solution)/shard_map/dot_general | solution.py:24
  299.7 1.5 multiply_convert_fusion
  301.6 1.4 copy.87
  303.7 0.9 tanh.11
  304.6 1.1 subtract_multiply_fusion
  305.7 0.9 reshape.315
  306.6 1.1 dot_general.122
  307.7 0.9 copy.89
  308.6 8.3 %multiply_reduce_fusion = (f32[128,64]{0,1:T(8,128)S(1)}, f32[128,64,128]{2,0,1:T(8,128)S(1)}) fusion(f32[128,64,128]{2,0,1:T(8,128)} %copy-done.6, f32[128,64]{0,1:T(8,128)} %copy-done.23, f32[128,64,6]{0,2,1:T(8,128)} %copy.89, bf16[128,6]{0,1:T(8,128)(2,1)S(1)} %copy-done.36), kind=kOutput, calls=%fused_computation.14 | convolution fusion | flops 87023616 | bytes 8652288 | tf_op jit(solution)/shard_map/dot_general | solution.py:86
  316.9 2.5 subtract_convert_fusion
  319.4 1.4 fusion.64
  320.8 1.4 fusion.76
  322.5 1.4 fusion.79
  324.7 1.9 collective-permute-start.5
  326.6 6.0 %collective-permute-start.4 = (bf16[1,64,128]{2,0,1:T(2,128)(2,1)S(1)}, bf16[1,64,128]{2,0,1:T(2,128)(2,1)S(1)}, u32[]{:S(2)}, u32[]{:S(2)}) collective-permute-start(bf16[1,64,128]{2,0,1:T(2,128)(2,1)S(1)} %get-tuple-element.31), channel_id=1, source_target_pairs={{0,32},{32,64},{64,96},{1,33},{33,65},{65,97},{2,34},{34,66},{66,9... | collective-permute-start | bytes 49160 | tf_op jit(solution)/shard_map/ppermute | solution.py:14
  332.7 1.4 fusion.63
  334.2 1.3 collective-permute-start.6
  335.5 4.3 collective-permute-start.7
  340.5 2.8 fusion.11
  343.2 3.6 maximum_maximum_fusion.1
  346.8 2.7 fusion.13
  349.5 2.7 fusion.17
  352.2 2.7 fusion.15
  354.9 2.8 fusion.19
  357.7 2.7 fusion.23
  360.4 10.8 %add_convert_fusion = bf16[128,64,128]{2,0,1:T(8,128)(2,1)} fusion(f32[128,64,128]{2,0,1:T(8,128)} %fusion.11, f32[128,64,128]{2,0,1:T(8,128)} %fusion.13, f32[128,64,128]{2,0,1:T(8,128)} %fusion.15, f32[128,64,128]{2,0,1:T(8,128)S(1)} %fusion.104, f32[128,64,128]{2,0,1:T(8,128)} %fusion.17, f32[128,64,128]{2,0,1:T(8,128)} %fusion.19, ...), kind=kOutput, calls=%fused_computation.12 | convolution fusion | flops 277872640 | bytes 37781504 | tf_op jit(solution)/shard_map/dot_general | solution.py:24
  371.2 3.0 copy.90
  374.2 29.2 %gather_fusion.3 = bf16[8192,128]{1,0:T(8,128)(2,1)} fusion(bf16[8192,128]{1,0:T(8,128)(2,1)S(1)} %bitcast.151, s32[8192]{0:T(1024)S(1)} %copy-done.28), kind=kCustom, calls=%fused_computation.3 | custom fusion | bytes 4227072 | tf_op jit(solution)/shard_map/gather | solution.py:184
  403.4 13.2 %all-to-all-start.1 = ((bf16[128,64,128]{2,1,0:T(8,128)(2,1)}), bf16[128,64,128]{2,1,0:T(8,128)(2,1)}, u32[]{:S(2)}, u32[]{:S(2)}) async-start(bf16[128,64,128]{2,1,0:T(8,128)(2,1)} %bitcast.157), calls=%async_computation.1 | async-start | bytes 4194304 | tf_op jit(solution)/shard_map/all_to_all | solution.py:185
  416.9 3.1 fusion.62
  420.2 0.9 maximum_bitcast_fusion.2
  421.1 2.5 fusion.67
  424.4 0.8 copy-done.10
  426.8 2.4 fusion.82
  429.3 0.9 pad_maximum_fusion.16
  431.1 0.9 convolution_bitcast_fusion
  432.0 68.6 %psum.15 = f32[128,6]{0,1:T(8,128)} all-reduce(f32[128,6]{0,1:T(8,128)S(1)} %convolution_bitcast_fusion), channel_id=1, replica_groups=mesh['bx'=4,'by'=32] {'bx','by'}, use_global_device_ids=true, to_apply=%region_9.10 | all-reduce | flops 768 | bytes 6144 | tf_op jit(solution)/shard_map/psum | solution.py:189
  500.6 5.0 convert_multiply_fusion
  505.6 5.4 fusion.85
  511.1 2.0 multiply_reduce_fusion.2
  514.5 62.9 %all-reduce.2.cloned.1.call-done = f32[3,3,128,128]{3,2,1,0:T(8,128)} async-done(((f32[3,3,128,128]{3,2,1,0:T(8,128)}), f32[3,3,128,128]{3,2,1,0:T(8,128)}) %all-reduce.2.cloned.1.call-update) | async-done | bytes 589840 | tf_op jit(solution)/shard_map/psum | solution.py:189
  577.4 1.9 copy.118
  (129 shorter events, 13.4 us)
Async XLA Ops:
  7.2 145.3 %copy-start = (bf16[256,128]{1,0:T(8,128)(2,1)S(1)}, bf16[256,128]{1,0:T(8,128)(2,1)}, u32[]{:S(2)}) copy-start(bf16[256,128]{1,0:T(8,128)(2,1)} %param.13) | copy-start | bytes 196612
  7.2 1.9 copy-start.1
  54.7 0.7 copy-start.2
  55.4 45.7 %copy-start.20 = (f32[64,128]{1,0:T(8,128)S(1)}, f32[64,128]{1,0:T(8,128)}, u32[]{:S(2)}) copy-start(f32[64,128]{1,0:T(8,128)} %param.12) | copy-start | bytes 98308
  100.9 0.6 copy-start.25
  101.6 50.8 %copy-start.35 = (s32[1,128]{1,0:T(1,128)S(1)}, s32[1,128]{1,0:T(1,128)}, u32[]{:S(2)}) copy-start(s32[1,128]{1,0:T(1,128)} %param.16) | copy-start | bytes 1540
  101.6 50.9 %copy-start.29 = (bf16[128,256]{1,0:T(8,128)(2,1)S(1)}, bf16[128,256]{1,0:T(8,128)(2,1)}, u32[]{:S(2)}) copy-start(bf16[128,256]{1,0:T(8,128)(2,1)} %param.11) | copy-start | bytes 196612
  157.3 11.5 %copy-start.37 = (s32[6]{0:T(128)S(1)}, s32[6]{0:T(128)}, u32[]{:S(2)}) copy-start(s32[6]{0:T(128)} %param.20) | copy-start | bytes 76
  157.3 12.0 %copy-start.34 = (s32[1,128,64]{1,2,0:T(8,128)S(1)}, s32[1,128,64]{1,2,0:T(8,128)}, u32[]{:S(2)}) copy-start(s32[1,128,64]{1,2,0:T(8,128)} %param.17) | copy-start | bytes 98308
  157.3 12.3 %copy-start.27 = (f32[6,128,64]{1,2,0:T(8,128)S(1)}, f32[6,128,64]{1,2,0:T(8,128)}, u32[]{:S(2)}) copy-start(f32[6,128,64]{1,2,0:T(8,128)} %param.21) | copy-start | bytes 589828
  157.3 42.0 %all-to-all-start = ((bf16[128,64,128]{2,1,0:T(8,128)(2,1)}), bf16[128,64,128]{2,1,0:T(8,128)(2,1)S(1)}, u32[]{:S(2)}, u32[]{:S(2)}) async-start(bf16[128,64,128]{2,1,0:T(8,128)(2,1)} %get-tuple-element.36), calls=%async_computation | async-start | bytes 4194304 | tf_op jit(solution)/shard_map/all_to_all | solution.py:165
  245.7 7.8 %copy-start.18 = (bf16[3,3,128,128]{3,2,1,0:T(8,128)(2,1)S(1)}, bf16[3,3,128,128]{3,2,1,0:T(8,128)(2,1)}, u32[]{:S(2)}) copy-start(bf16[3,3,128,128]{3,2,1,0:T(8,128)(2,1)} %param.18) | copy-start | bytes 884740
  248.1 9.8 %copy-start.14 = (bf16[8192,128]{1,0:T(8,128)(2,1)}, bf16[8192,128]{1,0:T(8,128)(2,1)S(1)}, u32[]{:S(2)}) copy-start(bf16[8192,128]{1,0:T(8,128)(2,1)S(1)} %convert_element_type.50) | copy-start | bytes 6291460
  248.2 11.1 %collective-permute-start = (bf16[1,64,128]{2,0,1:T(2,128)(2,1)S(1)}, bf16[1,64,128]{2,0,1:T(2,128)(2,1)S(1)}, u32[]{:S(2)}, u32[]{:S(2)}) collective-permute-start(bf16[1,64,128]{2,0,1:T(2,128)(2,1)S(1)} %copy.81), channel_id=1, source_target_pairs={{0,32},{32,64},{64,96},{1,33},{33,65},{65,97},{2,34},{34,66},{66,9... | collective-permute-start | bytes 49160 | tf_op jit(solution)/shard_map/ppermute | solution.py:14
  251.5 7.8 %collective-permute-start.1 = (bf16[1,64,128]{2,0,1:T(2,128)(2,1)S(1)}, bf16[1,64,128]{2,0,1:T(2,128)(2,1)S(1)}, u32[]{:S(2)}, u32[]{:S(2)}) collective-permute-start(bf16[1,64,128]{2,0,1:T(2,128)(2,1)S(1)} %copy.82), channel_id=1, source_target_pairs={{32,0},{64,32},{96,64},{33,1},{65,33},{97,65},{34,2},{66,34},{98,6... | collective-permute-start | bytes 49160 | tf_op jit(solution)/shard_map/ppermute | solution.py:17
  259.3 73.4 %copy-start.5 = (bf16[128,64,128]{2,0,1:T(8,128)(2,1)}, bf16[128,64,128]{2,0,1:T(8,128)(2,1)S(1)}, u32[]{:S(2)}) copy-start(bf16[128,64,128]{2,0,1:T(8,128)(2,1)S(1)} %copy.83) | copy-start | bytes 6291460
  259.3 9.8 %copy-start.21 = (bf16[1,64,128]{2,0,1:T(2,128)(2,1)}, bf16[1,64,128]{2,0,1:T(2,128)(2,1)S(1)}, u32[]{:S(2)}) copy-start(bf16[1,64,128]{2,0,1:T(2,128)(2,1)S(1)} %collective-permute-done) | copy-start | bytes 49156
  259.3 9.7 %collective-permute-start.2 = (bf16[130,1,128]{2,0,1:T(8,128)(2,1)S(1)}, bf16[130,1,128]{2,0,1:T(8,128)(2,1)S(1)}, u32[]{:S(2)}, u32[]{:S(2)}) collective-permute-start(bf16[130,1,128]{2,0,1:T(8,128)(2,1)S(1)} %get-tuple-element.27), channel_id=1, source_target_pairs={{0,1},{1,2},{2,3},{3,4},{4,5},{5,6},{6,7},{7,8},{8,9},{9,10},{10,1... | collective-permute-start | bytes 99848 | tf_op jit(solution)/shard_map/ppermute | solution.py:14
  262.2 6.9 %collective-permute-start.3 = (bf16[130,1,128]{2,0,1:T(8,128)(2,1)S(1)}, bf16[130,1,128]{2,0,1:T(8,128)(2,1)S(1)}, u32[]{:S(2)}, u32[]{:S(2)}) collective-permute-start(bf16[130,1,128]{2,0,1:T(8,128)(2,1)S(1)} %get-tuple-element.26), channel_id=1, source_target_pairs={{1,0},{2,1},{3,2},{4,3},{5,4},{6,5},{7,6},{8,7},{9,8},{10,9},{11,1... | collective-permute-start | bytes 99848 | tf_op jit(solution)/shard_map/ppermute | solution.py:17
  272.3 8.5 %copy-start.8 = (bf16[130,65,128]{2,0,1:T(8,128)(2,1)}, bf16[130,65,128]{2,0,1:T(8,128)(2,1)S(1)}, u32[]{:S(2)}) copy-start(bf16[130,65,128]{2,0,1:T(8,128)(2,1)S(1)} %get-tuple-element.24) | copy-start | bytes 6489604
  272.3 11.2 %copy-start.11 = (bf16[130,65,128]{2,0,1:T(8,128)(2,1)}, bf16[130,65,128]{2,0,1:T(8,128)(2,1)S(1)}, u32[]{:S(2)}) copy-start(bf16[130,65,128]{2,0,1:T(8,128)(2,1)S(1)} %get-tuple-element.25) | copy-start | bytes 6489604
  299.6 2.0 copy-start.6
  299.6 2.0 copy-start.23
  301.6 1.4 copy-start.16
  301.6 1.4 copy-start.36
  308.6 8.3 %copy-start.7 = (f32[128,64,128]{2,0,1:T(8,128)S(1)}, f32[128,64,128]{2,0,1:T(8,128)}, u32[]{:S(2)}) copy-start(f32[128,64,128]{2,0,1:T(8,128)} %copy-done.6) | copy-start | bytes 12582916
  308.6 8.3 %copy-start.24 = (f32[128,64]{0,1:T(8,128)S(1)}, f32[128,64]{0,1:T(8,128)}, u32[]{:S(2)}) copy-start(f32[128,64]{0,1:T(8,128)} %copy-done.23) | copy-start | bytes 98308
  316.9 2.5 copy-start.12
  319.4 23.8 %copy-start.3 = (bf16[128,64,128]{2,0,1:T(8,128)(2,1)}, bf16[128,64,128]{2,0,1:T(8,128)(2,1)S(1)}, u32[]{:S(2)}) copy-start(bf16[128,64,128]{2,0,1:T(8,128)(2,1)S(1)} %subtract_convert_fusion) | copy-start | bytes 6291460
  320.8 1.6 copy-start.9
  322.5 1.5 copy-start.19
  324.0 8.7 %copy-start.22 = (bf16[1,64,128]{2,0,1:T(2,128)(2,1)S(1)}, bf16[1,64,128]{2,0,1:T(2,128)(2,1)}, u32[]{:S(2)}) copy-start(bf16[1,64,128]{2,0,1:T(2,128)(2,1)} %copy-done.21) | copy-start | bytes 49156
  324.7 9.4 %collective-permute-start.5 = (bf16[1,64,128]{2,0,1:T(2,128)(2,1)S(1)}, bf16[1,64,128]{2,0,1:T(2,128)(2,1)S(1)}, u32[]{:S(2)}, u32[]{:S(2)}) collective-permute-start(bf16[1,64,128]{2,0,1:T(2,128)(2,1)S(1)} %get-tuple-element.30), channel_id=1, source_target_pairs={{32,0},{64,32},{96,64},{33,1},{65,33},{97,65},{34,2},{66,34},{98,6... | collective-permute-start | bytes 49160 | tf_op jit(solution)/shard_map/ppermute | solution.py:17
  326.6 7.5 %collective-permute-start.4 = (bf16[1,64,128]{2,0,1:T(2,128)(2,1)S(1)}, bf16[1,64,128]{2,0,1:T(2,128)(2,1)S(1)}, u32[]{:S(2)}, u32[]{:S(2)}) collective-permute-start(bf16[1,64,128]{2,0,1:T(2,128)(2,1)S(1)} %get-tuple-element.31), channel_id=1, source_target_pairs={{0,32},{32,64},{64,96},{1,33},{33,65},{65,97},{2,34},{34,66},{66,9... | collective-permute-start | bytes 49160 | tf_op jit(solution)/shard_map/ppermute | solution.py:14
  334.2 9.1 %collective-permute-start.6 = (bf16[130,1,128]{2,0,1:T(8,128)(2,1)S(1)}, bf16[130,1,128]{2,0,1:T(8,128)(2,1)S(1)}, u32[]{:S(2)}, u32[]{:S(2)}) collective-permute-start(bf16[130,1,128]{2,0,1:T(8,128)(2,1)S(1)} %get-tuple-element.23), channel_id=1, source_target_pairs={{1,0},{2,1},{3,2},{4,3},{5,4},{6,5},{7,6},{8,7},{9,8},{10,9},{11,1... | collective-permute-start | bytes 99848 | tf_op jit(solution)/shard_map/ppermute | solution.py:17
  335.5 7.8 %collective-permute-start.7 = (bf16[130,1,128]{2,0,1:T(8,128)(2,1)S(1)}, bf16[130,1,128]{2,0,1:T(8,128)(2,1)S(1)}, u32[]{:S(2)}, u32[]{:S(2)}) collective-permute-start(bf16[130,1,128]{2,0,1:T(8,128)(2,1)S(1)} %get-tuple-element.22), channel_id=1, source_target_pairs={{0,1},{1,2},{2,3},{3,4},{4,5},{5,6},{6,7},{7,8},{8,9},{9,10},{10,1... | collective-permute-start | bytes 99848 | tf_op jit(solution)/shard_map/ppermute | solution.py:14
  371.2 3.0 copy-start.28
  403.4 13.5 %copy-start.4 = (bf16[128,64,128]{2,0,1:T(8,128)(2,1)S(1)}, bf16[128,64,128]{2,0,1:T(8,128)(2,1)}, u32[]{:S(2)}) copy-start(bf16[128,64,128]{2,0,1:T(8,128)(2,1)} %copy-done.3) | copy-start | bytes 6291460
  403.4 97.1 %all-to-all-start.1 = ((bf16[128,64,128]{2,1,0:T(8,128)(2,1)}), bf16[128,64,128]{2,1,0:T(8,128)(2,1)}, u32[]{:S(2)}, u32[]{:S(2)}) async-start(bf16[128,64,128]{2,1,0:T(8,128)(2,1)} %bitcast.157), calls=%async_computation.1 | async-start | bytes 4194304 | tf_op jit(solution)/shard_map/all_to_all | solution.py:185
  416.6 3.6 copy-start.32
  416.6 3.6 copy-start.33
  416.6 160.7 %all-reduce.2.cloned.1.call-start = ((), (), s32[]{:S(2)}) async-start(), calls=%async_computation.2 | async-start | bytes 1179648 | tf_op jit(solution)/shard_map/psum | solution.py:189
  421.1 2.5 copy-start.13
  423.6 1.6 copy-start.10
  425.2 1.6 copy-start.15
  426.8 2.5 copy-start.30
  426.8 2.5 copy-start.31
  429.3 1.8 copy-start.17
  505.6 5.5 copy-start.26
Sparse Core Ops, SparseCore 0:
  430.3 147.0 all-reduce.1
where the time goes:
time: 596 us; the launch traced here: 587 us
  local copies, waits for them, and re-layouts  189 us (32%)
  matrix products  104 us (17%)
  waiting for transfers between devices  91.7 us (15%)
  other arithmetic  70.8 us (12%)
  blocking collectives  68.6 us (12%)
  starting transfers between devices  48 us (8%)
  between operations  15.2 us (3%)
    psum x1, blocking collectives, per_device(): grad_conv, grad_proj = lax.psum((conv_part, proj_part), ('bx', 'by'))  68.6 us
    dot_general x18, matrix products, plane_dot(): jnp.dot(window.reshape(rows * cols, depth), weight, preferred_element_typ...  65.6 us
    psum x1, waiting for transfers between devices, per_device(): grad_conv, grad_proj = lax.psum((conv_part, proj_part), ('bx', 'by'))  62.9 us
    gather x2, local copies, waits for them, and re-layouts, slot_values(): point_weight = jnp.where(usable, depth_prob[depths, pixels], 0.0)  50.8 us
    scatter-add x1, other arithmetic, per_device(): jax.ops.segment_sum(arrived.reshape(-1, channels).astype(jnp.float32), ta...  46.4 us
    gather x2, local copies, waits for them, and re-layouts, slot_values(): pixels = pixel_list[slot_index]  45.6 us
    gather x2, local copies, waits for them, and re-layouts, slot_values(): depths = depth_list[slot_index]  45.6 us
    gather x1, local copies, waits for them, and re-layouts, per_device(): cell_grads = lift_grad[targets].reshape(tile_count, capacity, channels)  29.2 us
  transfers between devices with their start and end apart: 11, of which 2 were waited for; matrix products, arithmetic and copies ran while one was open for 8% of the time, Pallas kernels for 0%

commit v1 on v0

v1 whole, which is shorter than its diff:
```python
import functools

import jax
import jax.numpy as jnp
from jax import lax
from jax.experimental import pallas as pl
from jax.experimental.pallas import tpu as pltpu
from jax.sharding import PartitionSpec as P

epsilon = 1e-05
MESH = pl.DeviceIdType.MESH
F32 = jnp.float32
BF16 = jnp.bfloat16
VMEM_LIMIT = 60 * 2**20
NT = (((1,), (1,)), ((), ()))
TN = (((0,), (0,)), ((), ()))
PITCH = 80
DIRECTIONS = ((-1, 0), (1, 0), (0, -1), (0, 1), (-1, -1), (-1, 1), (1, -1), (1, 1))


def dot(left, right, dims=(((1,), (0,)), ((), ()))):
    return lax.dot_general(left, right, dims, preferred_element_type=F32)


def halves(value):
    high = value.astype(BF16)
    return high, (value - high.astype(F32)).astype(BF16)


def position():
    count = lax.axis_size("bx") * lax.axis_size("by")
    return lax.axis_index("bx") * lax.axis_size("by") + lax.axis_index("by"), count


def place(index):
    cols = lax.axis_size("by")
    return (lax.div(index, cols), lax.rem(index, cols))


def greet_all(me, count):
    barrier = pltpu.get_barrier_semaphore()

    def greet(step, carry):
        pl.semaphore_signal(
            barrier, inc=1, device_id=place(lax.rem(me + step, count)), device_id_type=MESH
        )
        return carry

    lax.fori_loop(1, count, greet, 0)
    return barrier


def lift_kernel(
    counts, features, logits, ctx_weight, pixels, bins,
    arrived, prob_out, ctx_out, weight_out,
    values, outgoing, starts, send_sem, recv_sem, own_sem,
):
    me, count = position()
    capacity = outgoing.shape[1]
    pix_count = ctx_out.shape[0]
    bin_count = prob_out.shape[0]
    barrier = greet_all(me, count)
    context = dot(features[...], ctx_weight[...]).astype(BF16)
    ctx_out[...] = context
    raw = logits[...]
    shifted = jnp.exp(raw - jnp.max(raw, axis=0, keepdims=True))
    prob = shifted / jnp.sum(shifted, axis=0, keepdims=True)
    prob_out[...] = prob
    prob_pair = jnp.concatenate(halves(prob), axis=1)
    ctx_pair = jnp.concatenate([context, context], axis=0)

    def start_of(tile, begin):
        starts[tile] = begin
        return begin + counts[0, tile]

    lax.fori_loop(0, count, start_of, 0)
    pix_lane = lax.broadcasted_iota(jnp.int32, (pix_count, 128), 0)
    bin_lane = lax.broadcasted_iota(jnp.int32, (bin_count, 128), 0)
    chunks = pixels.shape[0]
    group = 4

    def lift_chunk(step, carry):
        for part in range(group):
            chunk = step * group + part
            hot = pixels[pl.ds(chunk, 1), :] == pix_lane
            hot_b = jnp.where(hot, 1.0, 0.0).astype(BF16)
            picked = dot(prob_pair, jnp.concatenate([hot_b, hot_b], axis=0))
            weight = jnp.sum(
                jnp.where(bins[pl.ds(chunk, 1), :] == bin_lane, picked, 0.0), axis=0, keepdims=True
            )
            weight_out[pl.ds(chunk, 1), :] = weight
            spread = jnp.concatenate(halves(jnp.where(hot, weight, 0.0)), axis=0)
            values[pl.ds(pl.multiple_of(chunk * 128, 128), 128), :] = dot(spread, ctx_pair, TN)
        return carry

    lax.fori_loop(0, chunks // group, lift_chunk, 0)
    slot = lax.broadcasted_iota(jnp.int32, (capacity, 128), 0)
    values[pl.ds(chunks * 128, capacity), :] = jnp.zeros((capacity, 128), F32)

    def pack(tile):
        rows = values[pl.ds(starts[tile], capacity), :]
        outgoing[tile] = jnp.where(slot < counts[0, tile], rows, 0.0).astype(BF16)

    pl.semaphore_wait(barrier, count - 1)

    def send(step, carry):
        tile = lax.rem(me + step, count)
        pack(tile)
        pltpu.make_async_remote_copy(
            src_ref=outgoing.at[tile],
            dst_ref=arrived.at[me],
            send_sem=send_sem,
            recv_sem=recv_sem,
            device_id=place(tile),
            device_id_type=MESH,
        ).start()
        return carry

    lax.fori_loop(1, count, send, 0)
    pack(me)
    own = pltpu.make_async_copy(outgoing.at[me], arrived.at[me], own_sem)
    own.start()
    own.wait()
    others = pl.ds(0, count - 1)
    pltpu.make_async_copy(outgoing.at[others], outgoing.at[others], send_sem).wait()
    pltpu.make_async_copy(arrived.at[others], arrived.at[others], recv_sem).wait()


def lift(counts, features, logits, ctx_weight, pixels, bins, capacity):
    count = counts.shape[1]
    bin_count, pix_count = logits.shape
    channels = ctx_weight.shape[1]
    points = pixels.shape[0] * 128
    vmem = pl.BlockSpec(memory_space=pltpu.VMEM)
    return pl.pallas_call(
        lift_kernel,
        out_shape=(
            jax.ShapeDtypeStruct((count, capacity, channels), BF16),
            jax.ShapeDtypeStruct((bin_count, pix_count), F32),
            jax.ShapeDtypeStruct((pix_count, channels), BF16),
            jax.ShapeDtypeStruct(pixels.shape, F32),
        ),
        in_specs=[pl.BlockSpec(memory_space=pltpu.SMEM)] + [vmem] * 5,
        out_specs=(pl.BlockSpec(memory_space=pl.ANY), vmem, vmem, vmem),
        scratch_shapes=[
            pltpu.VMEM((points + capacity, channels), F32),
            pltpu.VMEM((count, capacity, channels), BF16),
            pltpu.SMEM((count,), jnp.int32),
            pltpu.SemaphoreType.DMA,
            pltpu.SemaphoreType.DMA,
            pltpu.SemaphoreType.DMA,
        ],
        compiler_params=pltpu.CompilerParams(
            collective_id=0, has_side_effects=True, vmem_limit_bytes=VMEM_LIMIT
        ),
        name="lift",
    )(counts, features, logits, ctx_weight, pixels, bins)


SUMS = 4


def pool_kernel(cells, arrived, lifted, *scratch):
    sums, stage = scratch[:SUMS], scratch[SUMS]
    count, capacity, channels = arrived.shape
    rows = lifted.shape[0]

    def clear(step, carry):
        at = pl.ds(pl.multiple_of(step * 128, 128), 128)
        for one in sums:
            one[at, :] = jnp.zeros((128, channels), F32)
        return carry

    lax.fori_loop(0, rows // 128, clear, 0)

    def add_block(sender, carry):
        stage[...] = arrived[sender].astype(F32)
        for slot in range(capacity):
            one = sums[slot % SUMS]
            cell = cells[sender, slot]
            one[pl.ds(cell, 1), :] = one[pl.ds(cell, 1), :] + stage[pl.ds(slot, 1), :]
        return carry

    lax.fori_loop(0, count, add_block, 0)

    def finish(step, carry):
        at = pl.ds(pl.multiple_of(step * 128, 128), 128)
        total = sums[0][at, :]
        for one in sums[1:]:
            total = total + one[at, :]
        lifted[at, :] = total.astype(BF16)
        return carry

    lax.fori_loop(0, rows // 128, finish, 0)


def pool(cells, arrived, rows):
    count, capacity, channels = arrived.shape
    vmem = pl.BlockSpec(memory_space=pltpu.VMEM)
    return pl.pallas_call(
        pool_kernel,
        out_shape=jax.ShapeDtypeStruct((rows, channels), BF16),
        in_specs=[pl.BlockSpec(memory_space=pltpu.SMEM), vmem],
        out_specs=vmem,
        scratch_shapes=[pltpu.VMEM((rows, channels), F32) for _ in range(SUMS)]
        + [pltpu.VMEM((capacity, channels), F32)],
        compiler_params=pltpu.CompilerParams(vmem_limit_bytes=VMEM_LIMIT),
        name="pool",
    )(cells, arrived)


def point_kernel(
    counts, back, prob, context, weights, pixels, bins, ctx_weight,
    logit_grad, feature_grad,
    grads,
):
    count, capacity, channels = back.shape
    pix_count = context.shape[0]
    bin_count = prob.shape[0]

    def unpack(tile, begin):
        grads[pl.ds(begin, capacity), :] = back[tile].astype(F32)
        return begin + counts[0, tile]

    lax.fori_loop(0, count, unpack, 0)
    pix_lane = lax.broadcasted_iota(jnp.int32, (pix_count, 128), 0)
    bin_lane = lax.broadcasted_iota(jnp.int32, (bin_count, 128), 0)
    chunks = pixels.shape[0]
    group = 4
    ctx = context[...]

    def chunk_grads(step, carry):
        prob_grad, ctx_grad = carry
        for part in range(group):
            chunk = step * group + part
            grad = grads[pl.ds(pl.multiple_of(chunk * 128, 128), 128), :].astype(BF16)
            hot = pixels[pl.ds(chunk, 1), :] == pix_lane
            hot_b = jnp.where(hot, 1.0, 0.0).astype(BF16)
            pair = jnp.sum(jnp.where(hot, dot(ctx, grad, NT), 0.0), axis=0, keepdims=True)
            by_bin = jnp.where(bins[pl.ds(chunk, 1), :] == bin_lane, pair, 0.0)
            prob_grad = prob_grad + dot(
                jnp.concatenate(halves(by_bin), axis=1), jnp.concatenate([hot_b, hot_b], axis=1), NT
            )
            spread = jnp.concatenate(
                halves(jnp.where(hot, weights[pl.ds(chunk, 1), :], 0.0)), axis=1
            )
            ctx_grad = ctx_grad + dot(spread, jnp.concatenate([grad, grad], axis=0))
        return prob_grad, ctx_grad

    prob_grad, ctx_grad = lax.fori_loop(
        0,
        chunks // group,
        chunk_grads,
        (jnp.zeros((bin_count, pix_count), F32), jnp.zeros((pix_count, channels), F32)),
    )
    chance = prob[...]
    logit_grad[...] = chance * (prob_grad - jnp.sum(chance * prob_grad, axis=0, keepdims=True))
    feature_grad[...] = dot(ctx_grad.astype(BF16), ctx_weight[...], NT).astype(BF16)


def point_grads(counts, back, prob, context, weights, pixels, bins, ctx_weight):
    vmem = pl.BlockSpec(memory_space=pltpu.VMEM)
    capacity, channels = back.shape[1:]
    return pl.pallas_call(
        point_kernel,
        out_shape=(
            jax.ShapeDtypeStruct(prob.shape, F32),
            jax.ShapeDtypeStruct((context.shape[0], ctx_weight.shape[0]), BF16),
        ),
        in_specs=[pl.BlockSpec(memory_space=pltpu.SMEM)] + [vmem] * 7,
        out_specs=(vmem, vmem),
        scratch_shapes=[pltpu.VMEM((pixels.shape[0] * 128 + capacity, channels), F32)],
        compiler_params=pltpu.CompilerParams(vmem_limit_bytes=VMEM_LIMIT),
        name="point_grads",
    )(counts, back, prob, context, weights, pixels, bins, ctx_weight)


def grid_place():
    return lax.axis_index("bx"), lax.axis_index("by"), lax.axis_size("bx"), lax.axis_size("by")


def inside(dx, dy):
    bx, by, nx, ny = grid_place()
    x, y = bx + dx, by + dy
    return (x >= 0) & (x < nx) & (y >= 0) & (y < ny)


def halo_copies(top, bottom, sides, landed, send_sems, recv_sems):
    bx, by, _, _ = grid_place()
    depth = sides.shape[1]
    pieces = (
        (top, landed.at[0, pl.ds(0, top.shape[0])]),
        (bottom, landed.at[1, pl.ds(0, bottom.shape[0])]),
        (sides.at[0], landed.at[2]),
        (sides.at[1], landed.at[3]),
        (sides.at[0, pl.ds(0, 16)], landed.at[4, pl.ds(0, 16)]),
        (sides.at[1, pl.ds(0, 16)], landed.at[5, pl.ds(0, 16)]),
        (sides.at[0, pl.ds(depth - 16, 16)], landed.at[6, pl.ds(0, 16)]),
        (sides.at[1, pl.ds(depth - 16, 16)], landed.at[7, pl.ds(0, 16)]),
    )
    return [
        pltpu.make_async_remote_copy(
            src_ref=source,
            dst_ref=target,
            send_sem=send_sems.at[way],
            recv_sem=recv_sems.at[way],
            device_id=(bx + dx, by + dy),
            device_id_type=MESH,
        )
        for way, ((dx, dy), (source, target)) in enumerate(zip(DIRECTIONS, pieces))
    ]


def start_halo(copies):
    for (dx, dy), copy in zip(DIRECTIONS, copies):
        pl.when(inside(dx, dy))(copy.start)


def finish_halo(copies, landed, field, rows, cols):
    low = (rows + 1) * PITCH

    def lay(way):
        if way == 0:
            field[pl.ds(low + 8, cols), :] = landed[0, 0:cols].astype(F32)
        elif way == 1:
            field[pl.ds(8, cols), :] = landed[1, 0:cols].astype(F32)
        elif way == 2:
            field[pl.ds(PITCH + 8 + cols, rows, stride=PITCH), :] = landed[2].astype(F32)
        elif way == 3:
            field[pl.ds(PITCH + 7, rows, stride=PITCH), :] = landed[3].astype(F32)
        elif way == 4:
            field[pl.ds(low + 8 + cols, 1), :] = landed[4, 0:16].astype(F32)[0:1]
        elif way == 5:
            field[pl.ds(low + 7, 1), :] = landed[5, 0:16].astype(F32)[0:1]
        elif way == 6:
            field[pl.ds(8 + cols, 1), :] = landed[6, 0:16].astype(F32)[15:16]
        else:
            field[pl.ds(7, 1), :] = landed[7, 0:16].astype(F32)[15:16]

    for way, ((dx, dy), copy) in enumerate(zip(DIRECTIONS, copies)):

        def arrive(way=way, copy=copy):
            copy.wait_recv()
            lay(way)

        pl.when(inside(-dx, -dy))(arrive)
        pl.when(inside(dx, dy))(copy.wait_send)


def spread_columns(field, wide, rows, cols):
    channels = field.shape[1]

    def row(x, carry):
        base = pl.multiple_of(x * PITCH, 8)
        at = pl.ds(pl.multiple_of(x * cols, cols), cols)
        for shift in range(3):
            wide[at, pl.ds(shift * channels, channels)] = field[
                pl.ds(base + 7 + shift, cols), :
            ].astype(BF16)
        return carry

    lax.fori_loop(0, rows + 2, row, 0)


def tile_kernel(
    cells, lifted, weight, back_weight, proj, levels, code_grad,
    codes, back, sums_out,
    field, wide, wide_grad, lift_grad, sides, edges, landed, stage, outgoing, parts, gathered,
    halo_send, halo_recv, send_sem, recv_sem, part_send, part_recv, sum_send, sum_recv, own_sem,
):
    me, count = position()
    channels = lifted.shape[1]
    capacity = outgoing.shape[1]
    cols = edges.shape[1]
    rows = lifted.shape[0] // cols
    owners = parts.shape[0]
    code_dims = code_grad.shape[0]
    barrier = greet_all(me, count)

    zeros = jnp.zeros((PITCH, channels), F32)
    field[pl.ds(0, PITCH), :] = zeros
    field[pl.ds((rows + 1) * PITCH, PITCH), :] = zeros
    for column in (7, 8 + cols):
        field[pl.ds(PITCH + column, rows, stride=PITCH), :] = jnp.zeros((rows, channels), F32)

    def load_row(x, carry):
        field[pl.ds(pl.multiple_of((x + 1) * PITCH + 8, 8), cols), :] = lifted[
            pl.ds(pl.multiple_of(x * cols, cols), cols), :
        ].astype(F32)
        return carry

    lax.fori_loop(0, rows, load_row, 0)

    def fill_borders():
        sides[0] = field[pl.ds(PITCH + 8, rows, stride=PITCH), :].astype(BF16)
        sides[1] = field[pl.ds(PITCH + 7 + cols, rows, stride=PITCH), :].astype(BF16)
        edges[0] = field[pl.ds(PITCH + 8, cols), :].astype(BF16)
        edges[1] = field[pl.ds(rows * PITCH + 8, cols), :].astype(BF16)

    fill_borders()
    pl.semaphore_wait(barrier, count - 1)
    first = halo_copies(
        edges.at[0], edges.at[1], sides, landed.at[0], halo_send.at[0], halo_recv.at[0]
    )
    start_halo(first)
    finish_halo(first, landed.at[0], field, rows, cols)
    spread_columns(field, wide, rows, cols)

    block_rows = 8
    block = block_rows * cols
    half_levels = (levels[...].astype(F32) - 1.0) * 0.5
    proj_pair = proj[...]
    depth = 3 * channels

    def encode(step, proj_sum):
        origin = pl.multiple_of(step * block, block)
        conv_out = jnp.zeros((block, channels), F32)
        for tap in range(3):
            window = wide[pl.ds(origin + tap * cols, block), :]
            conv_out = conv_out + dot(window, weight[pl.ds(tap * depth, depth), :])
        inv_rms = lax.rsqrt(jnp.mean(conv_out * conv_out, axis=-1, keepdims=True) + epsilon)
        normed = conv_out * inv_rms
        gate = 1.0 / (1.0 + jnp.exp(-normed))
        hidden = (normed * gate).astype(BF16)
        squash = jnp.tanh(dot(proj_pair, hidden, NT)[:code_dims])
        codes[:, pl.ds(origin, block)] = half_levels * squash
        slope = code_grad[:, pl.ds(origin, block)] * half_levels * (1.0 - squash * squash)
        slope_high = slope.astype(BF16).astype(F32)
        slope_pair = jnp.concatenate([slope_high, slope - slope_high], axis=0).astype(BF16)
        proj_two = dot(slope_pair, hidden)
        proj_sum = proj_sum + proj_two[:code_dims] + proj_two[code_dims:]
        hidden_grad = dot(slope_pair, proj_pair, TN)
        norm_grad = hidden_grad * (gate * (1.0 + normed * (1.0 - gate)))
        mixed = jnp.mean(norm_grad * normed, axis=-1, keepdims=True)
        conv_grad = inv_rms * (norm_grad - normed * mixed)
        for r in range(block_rows):
            at = pl.multiple_of((step * block_rows + r + 1) * PITCH + 8, 8)
            field[pl.ds(at, cols), :] = conv_grad[r * cols : (r + 1) * cols]
        wide_grad[pl.ds(origin + cols, block), pl.ds(channels, channels)] = conv_grad.astype(BF16)
        return proj_sum

    proj_sum = lax.fori_loop(
        0, rows // block_rows, encode, jnp.zeros((code_dims, channels), F32)
    )
    fill_borders()
    second = halo_copies(
        edges.at[0], edges.at[1], sides, landed.at[1], halo_send.at[1], halo_recv.at[1]
    )
    start_halo(second)

    for tap in range(3):
        for third in range(3):
            first_part = (tap * 3 + third) * (channels // 16)
            span = 2048

            def add(step, total, tap=tap, third=third):
                origin = pl.multiple_of(step * span, span)
                window = wide[
                    pl.ds(origin + tap * cols, span), pl.ds(third * channels, channels)
                ]
                grad = wide_grad[pl.ds(origin + cols, span), pl.ds(channels, channels)]
                return total + dot(window, grad, TN)

            total = lax.fori_loop(
                0, rows * cols // span, add, jnp.zeros((channels, channels), F32)
            )
            parts[pl.ds(first_part, channels // 16)] = total.reshape(channels // 16, 16, channels)
    parts[owners - 1] = jnp.concatenate(
        [proj_sum, jnp.zeros((16 - code_dims, channels), F32)], axis=0
    )

    def share_of(device):
        return lax.rem(device * 45, count)

    def send_part(step, carry):
        target = lax.rem(me + step, count)
        share = share_of(target)

        @pl.when(share < owners)
        def _():
            pltpu.make_async_remote_copy(
                src_ref=parts.at[share],
                dst_ref=gathered.at[me],
                send_sem=part_send,
                recv_sem=part_recv,
                device_id=place(target),
                device_id_type=MESH,
            ).start()

        return carry

    lax.fori_loop(1, count, send_part, 0)

    finish_halo(second, landed.at[1], field, rows, cols)
    spread_columns(field, wide_grad, rows, cols)

    def conv_back(step, carry):
        origin = pl.multiple_of(step * block, block)
        total = jnp.zeros((block, channels), F32)
        for tap in range(3):
            window = wide_grad[pl.ds(origin + tap * cols, block), :]
            total = total + dot(window, back_weight[pl.ds(tap * depth, depth), :])
        lift_grad[pl.ds(origin, block), :] = total
        return carry

    lax.fori_loop(0, rows // block_rows, conv_back, 0)

    def pick(sender):
        for slot in range(capacity):
            stage[pl.ds(slot, 1), :] = lift_grad[pl.ds(cells[sender, slot], 1), :]
        outgoing[sender] = stage[...].astype(BF16)

    def send_back(step, carry):
        sender = lax.rem(me + step, count)
        pick(sender)
        pltpu.make_async_remote_copy(
            src_ref=outgoing.at[sender],
            dst_ref=back.at[me],
            send_sem=send_sem,
            recv_sem=recv_sem,
            device_id=place(sender),
            device_id_type=MESH,
        ).start()
        return carry

    lax.fori_loop(1, count, send_back, 0)
    pick(me)
    own = pltpu.make_async_copy(outgoing.at[me], back.at[me], own_sem)
    own.start()

    mine = share_of(me)
    others = pl.ds(0, count - 1)

    @pl.when(mine < owners)
    def _():
        pltpu.make_async_copy(gathered.at[others], gathered.at[others], part_recv).wait()
        gathered[me] = parts[mine]

        def add(source, total):
            return total + gathered[source]

        sums_out[mine] = lax.fori_loop(0, count, add, jnp.zeros((16, channels), F32))

        def send_sum(step, carry):
            pltpu.make_async_remote_copy(
                src_ref=sums_out.at[mine],
                dst_ref=sums_out.at[mine],
                send_sem=sum_send,
                recv_sem=sum_recv,
                device_id=place(lax.rem(me + step, count)),
                device_id_type=MESH,
            ).start()
            return carry

        lax.fori_loop(1, count, send_sum, 0)
        pltpu.make_async_copy(gathered.at[others], gathered.at[others], sum_send).wait()
        rest = pl.ds(0, owners - 1)
        pltpu.make_async_copy(parts.at[rest], parts.at[rest], part_send).wait()
        pltpu.make_async_copy(sums_out.at[rest], sums_out.at[rest], sum_recv).wait()

    @pl.when(mine >= owners)
    def _():
        pltpu.make_async_copy(parts, parts, part_send).wait()
        pltpu.make_async_copy(sums_out, sums_out, sum_recv).wait()

    own.wait()
    pltpu.make_async_copy(outgoing.at[others], outgoing.at[others], send_sem).wait()
    pltpu.make_async_copy(back.at[others], back.at[others], recv_sem).wait()


def tile_step(cells, lifted, weight, back_weight, proj, levels, code_grad, cols):
    count, capacity = cells.shape
    cells_all, channels = lifted.shape
    rows = cells_all // cols
    owners = weight.shape[0] // 16 + 1
    code_dims = code_grad.shape[0]
    vmem = pl.BlockSpec(memory_space=pltpu.VMEM)
    wide = pltpu.VMEM(((rows + 2) * cols, 3 * channels), BF16)
    return pl.pallas_call(
        tile_kernel,
        out_shape=(
            jax.ShapeDtypeStruct((code_dims, cells_all), F32),
            jax.ShapeDtypeStruct((count, capacity, channels), BF16),
            jax.ShapeDtypeStruct((owners, 16, channels), F32),
        ),
        in_specs=[pl.BlockSpec(memory_space=pltpu.SMEM)] + [vmem] * 6,
        out_specs=(vmem, pl.BlockSpec(memory_space=pl.ANY), vmem),
        scratch_shapes=[
            pltpu.VMEM(((rows + 2) * PITCH, channels), F32),
            wide,
            wide,
            pltpu.VMEM((cells_all, channels), F32),
            pltpu.VMEM((2, rows, channels), BF16),
            pltpu.VMEM((2, cols, channels), BF16),
            pltpu.VMEM((2, 8, rows, channels), BF16),
            pltpu.VMEM((capacity, channels), F32),
            pltpu.VMEM((count, capacity, channels), BF16),
            pltpu.VMEM((owners, 16, channels), F32),
            pltpu.VMEM((count, 16, channels), F32),
            pltpu.SemaphoreType.DMA((2, 8)),
            pltpu.SemaphoreType.DMA((2, 8)),
        ]
        + [pltpu.SemaphoreType.DMA] * 7,
        compiler_params=pltpu.CompilerParams(
            collective_id=1, has_side_effects=True, vmem_limit_bytes=VMEM_LIMIT
        ),
        name="tile_step",
    )(cells, lifted, weight, back_weight, proj, levels, code_grad)


def per_device(
    features,
    depth_logits,
    ctx_weight,
    point_pixel,
    point_bin,
    segment_count,
    slot_cell,
    conv_weight,
    proj_weight,
    level_count,
    code_grad,
):
    capacity = slot_cell.shape[2]
    code_dims, tile_rows, tile_cols = code_grad.shape
    channels = ctx_weight.shape[1]
    pixels = point_pixel.reshape(-1, 128)
    bins = point_bin.reshape(-1, 128)
    arrived, prob, context, weights = lift(
        segment_count, features, depth_logits, ctx_weight, pixels, bins, capacity
    )
    cells = slot_cell[0]
    lifted = pool(cells, arrived, tile_rows * tile_cols)
    spare = 8 - code_dims
    weight = conv_weight.reshape(9 * channels, channels)
    back_weight = conv_weight[::-1, ::-1].transpose(0, 1, 3, 2).reshape(9 * channels, channels)
    proj = jnp.pad(proj_weight.T, ((0, spare), (0, 0)))
    levels = jnp.pad(level_count, (0, spare), constant_values=1).reshape(8, 1)
    slopes = jnp.pad(code_grad.reshape(code_dims, -1), ((0, spare), (0, 0)))
    codes, back, sums = tile_step(
        cells,
        lifted,
        weight,
        back_weight,
        jnp.concatenate([proj, proj], axis=0),
        levels,
        slopes,
        tile_cols,
    )
    grad_logits, grad_features = point_grads(
        segment_count, back, prob, context, weights, pixels, bins, ctx_weight
    )
    grad_conv = sums[:-1].reshape(conv_weight.shape)
    grad_proj = sums[-1, :code_dims].T
    fsq_codes = codes[:code_dims].reshape(code_dims, tile_rows, tile_cols)
    return (fsq_codes, grad_logits, grad_features, grad_conv, grad_proj)


def solution(mesh):
    return jax.shard_map(
        per_device,
        mesh=mesh,
        in_specs=(
            P(("bx", "by"), None),
            P(None, ("bx", "by")),
            P(),
            P(("bx", "by")),
            P(("bx", "by")),
            P(("bx", "by"), None),
            P(("bx", "by"), None, None),
            P(),
            P(),
            P(),
            P(None, "bx", "by"),
        ),
        out_specs=(P(None, "bx", "by"), P(None, ("bx", "by")), P(("bx", "by"), None), P(), P()),
        check_vma=False,
    )
```

time: 596 us -> 173 us (0.29); the launches traced: 587 us -> 172 us
  local copies, waits for them, and re-layouts: 189 us -> 11.5 us
  Pallas kernels: 0 us -> 159 us
  matrix products: 104 us -> 0 us
  waiting for transfers between devices: 91.7 us -> 0 us
  other arithmetic: 70.8 us -> 0.6 us
  blocking collectives: 68.6 us -> 0 us
  starting transfers between devices: 48 us -> 0 us
  between operations: 15.2 us -> 0.68 us
    gather x7 -> x0, local copies, waits for them, and re-layouts: 171 us -> none  [the longest x2 50.8 us: slot_values(): point_weight = jnp.where(usable, depth_prob[depths, pixels], 0.0)]
    pallas_call x0 -> x4, Pallas kernels: none -> 159 us  [the longest x1 94.5 us: tile_step(): pl.pallas_call(tile_kernel, out_shape=(jax.ShapeDtypeStruct((code_dims, c...]
    dot_general x34 -> x0, matrix products: 104 us -> none  [the longest x18 65.6 us: plane_dot(): jnp.dot(window.reshape(rows * cols, depth), weight, preferred_element_typ...]
    psum x1 -> x0, blocking collectives: 68.6 us -> none  [per_device(): grad_conv, grad_proj = lax.psum((conv_part, proj_part), ('bx', 'by'))]
    psum x1 -> x0, waiting for transfers between devices: 62.9 us -> none  [per_device(): grad_conv, grad_proj = lax.psum((conv_part, proj_part), ('bx', 'by'))]
    scatter-add x1 -> x0, other arithmetic: 46.4 us -> none  [per_device(): jax.ops.segment_sum(arrived.reshape(-1, channels).astype(jnp.float32), ta...]
    all_to_all x2 -> x0, waiting for transfers between devices: 28.8 us -> none  [the longest x1 28.8 us: per_device(): lax.all_to_all(carried, ('bx', 'by'), split_axis=0, concat_axis=0, tiled=...]
    all_to_all x2 -> x0, starting transfers between devices: 24.7 us -> none  [the longest x1 13.2 us: per_device(): lax.all_to_all(cell_grads, ('bx', 'by'), split_axis=0, concat_axis=0, til...]
  transfers between devices with their start and end apart: 11 -> 0, of which waited for: 2 -> 0; matrix products, arithmetic and copies ran while one was open for 8% -> 0% of each run, Pallas kernels for 0% -> 0%
where the time goes in v1:
time: 173 us; the launch traced here: 172 us
  Pallas kernels  159 us (92%)
  local copies, waits for them, and re-layouts  11.5 us (7%)
    pallas_call x1, Pallas kernels, tile_step(): pl.pallas_call(tile_kernel, out_shape=(jax.ShapeDtypeStruct((code_dims, c...  94.5 us
    pallas_call x1, Pallas kernels, lift(): pl.pallas_call(lift_kernel, out_shape=(jax.ShapeDtypeStruct((count, capac...  41.1 us
    pallas_call x1, Pallas kernels, pool(): pl.pallas_call(pool_kernel, out_shape=jax.ShapeDtypeStruct((rows, channel...  15.9 us
    pallas_call x1, Pallas kernels, point_grads(): pl.pallas_call(point_kernel, out_shape=(jax.ShapeDtypeStruct(prob.shape,...  7.91 us

profile of v1, /device:TPU:1, one launch (start us, length us, event | category | flops | bytes accessed | tf_op | source)
XLA Modules:
  0.0 172.3 jit_solution(3451795975187666091)
XLA Ops:
  0.6 0.7 pad_bitcast_fusion
  1.3 0.7 pad.12
  2.0 0.6 pad_maximum_fusion.proj
  2.6 0.7 copy.24.levels
  3.2 1.5 copy.21
  4.7 1.0 reverse_bitcast_fusion
  5.7 0.9 copy.22
  6.6 1.1 copy.23
  7.7 0.1 reshape.39
  7.9 0.7 pad.14.code_grad
  8.6 41.1 %lift.1 = (bf16[128,64,128]{2,1,0:T(8,128)(2,1)}, f32[64,128]{1,0:T(8,128)}, bf16[128,128]{1,0:T(8,128)(2,1)}, f32[32,128]{1,0:T(8,128)}) custom-call(s32[1,128]{1,0:T(1,128)} %counts.3, bf16[128,256]{1,0:T(8,128)(2,1)} %features.1, f32[64,128]{1,0:T(8,128)} %logits.1, bf16[256,128]{1,0:T(8,128)(2,1)} %ctx_weight.3, s32[32,128]{1,0:T(8,128)} %bitcast.22, ...), custom_call_target="tpu_custom_call" | custom-call | tf_op jit(solution)/shard_map/lift/pallas_call | solution.py:135
  49.7 15.9 %pool.1.lifted = bf16[8192,128]{1,0:T(8,128)(2,1)} custom-call(s32[128,64]{1,0:T(8,128)} %bitcast.18, bf16[128,64,128]{2,1,0:T(8,128)(2,1)} %get-tuple-element.14.arrived), custom_call_target="tpu_custom_call" | custom-call | tf_op jit(solution)/shard_map/pool/pallas_call | solution.py:200
  65.6 94.5 %tile_step.1 = (f32[8,8192]{1,0:T(8,128)}, bf16[128,64,128]{2,1,0:T(8,128)(2,1)}, f32[73,16,128]{2,1,0:T(8,128)}) custom-call(s32[128,64]{1,0:T(8,128)} %bitcast.19, bf16[8192,128]{1,0:T(8,128)(2,1)} %pool.1.lifted, bf16[1152,128]{1,0:T(8,128)(2,1)} %bitcast.16, bf16[1152,128]{1,0:T(8,128)(2,1)} %bitcast.17, bf16[16,128]{1,0:T(8,128)(2,1)} %pad_maximum_fusion.proj, ...), custom_call_target="tpu_custom_call" | custom-call | tf_op jit(solution)/shard_map/tile_step/pallas_call | solution.py:579
  160.1 0.0 copy-start
  160.1 1.3 slice_bitcast_fusion
  161.4 1.9 %slice.10 = f32[72,16,128]{2,1,0:T(8,128)} slice(f32[73,16,128]{2,1,0:T(8,128)} %get-tuple-element.22), slice={[0:72], [0:16], [0:128]} | slice | bytes 1179648 | tf_op jit(solution)/shard_map/slice | solution.py:653
  163.4 7.9 %point_grads.1 = (f32[64,128]{1,0:T(8,128)}, bf16[128,256]{1,0:T(8,128)(2,1)}) custom-call(s32[1,128]{1,0:T(1,128)} %counts.3, bf16[128,64,128]{2,1,0:T(8,128)(2,1)} %get-tuple-element.16.back, f32[64,128]{1,0:T(8,128)} %get-tuple-element.17.prob, bf16[128,128]{1,0:T(8,128)(2,1)} %get-tuple-element.18.context, f32[32,128]{1,0:T(8,128)} %get-tuple-element.19.weights, ...), custom_call_target="tpu_custom_call" | custom-call | tf_op jit(solution)/shard_map/point_grads/pallas_call | solution.py:264
  171.3 0.0 copy-done
  171.3 0.1 reshape.40
  171.4 0.8 copy.25
Async XLA Ops:
  160.1 11.2 %copy-start = (f32[8,8192]{1,0:T(8,128)S(1)}, f32[8,8192]{1,0:T(8,128)}, u32[]{:S(2)}) copy-start(f32[8,8192]{1,0:T(8,128)} %get-tuple-element.15) | copy-start | bytes 786436

commit v2 on v0

v2 whole, which is shorter than its diff:
```python
import jax
import jax.numpy as jnp
from jax import lax
from jax.experimental import pallas as pl
from jax.experimental.pallas import tpu as pltpu
from jax.sharding import PartitionSpec as P

epsilon = 1e-05
MESH = pl.DeviceIdType.MESH
F32 = jnp.float32
BF16 = jnp.bfloat16
I32 = jnp.int32
VMEM_LIMIT = 60 * 2**20
NT = (((1,), (1,)), ((), ()))
TN = (((0,), (0,)), ((), ()))
LANES = 128
PITCH = 80
STRIDE = 45
GROUP = 8
FOLD = 8
ENCODE_ROWS = 64
BACK_ROWS = 64
SPAN = 2048
SHARE = 16
SHARE_STRIDE = 45
DIRECTIONS = ((-1, 0), (1, 0), (0, -1), (0, 1), (-1, -1), (-1, 1), (1, -1), (1, 1))


def dot(left, right, dims=(((1,), (0,)), ((), ()))):
    return lax.dot_general(left, right, dims, preferred_element_type=F32)


def halves(value):
    high = value.astype(BF16)
    return high, (value - high.astype(F32)).astype(BF16)


def place(index):
    cols = lax.axis_size("by")
    return (lax.div(index, cols), lax.rem(index, cols))


def grid_place():
    return lax.axis_index("bx"), lax.axis_index("by"), lax.axis_size("bx"), lax.axis_size("by")


def inside(dx, dy):
    bx, by, nx, ny = grid_place()
    x, y = bx + dx, by + dy
    return (x >= 0) & (x < nx) & (y >= 0) & (y < ny)


def lane_iota(rows):
    return lax.broadcasted_iota(I32, (rows, LANES), 1)


def row_iota(rows):
    return lax.broadcasted_iota(I32, (rows, LANES), 0)


def halo_copies(edges, sides, landed, send_sems, recv_sems):
    bx, by, _, _ = grid_place()
    cols = edges.shape[1]
    depth = sides.shape[1]
    first, last = pl.ds(0, 16), pl.ds(depth - 16, 16)
    pieces = (
        (edges.at[0], landed.at[0, pl.ds(0, cols)]),
        (edges.at[1], landed.at[1, pl.ds(0, cols)]),
        (sides.at[0], landed.at[2]),
        (sides.at[1], landed.at[3]),
        (sides.at[0, first], landed.at[4, first]),
        (sides.at[1, first], landed.at[5, first]),
        (sides.at[0, last], landed.at[6, first]),
        (sides.at[1, last], landed.at[7, first]),
    )
    return [
        pltpu.make_async_remote_copy(
            src_ref=source,
            dst_ref=target,
            send_sem=send_sems.at[way],
            recv_sem=recv_sems.at[way],
            device_id=(bx + dx, by + dy),
            device_id_type=MESH,
        )
        for way, ((dx, dy), (source, target)) in enumerate(zip(DIRECTIONS, pieces))
    ]


def start_halo(copies):
    for (dx, dy), copy in zip(DIRECTIONS, copies):
        pl.when(inside(dx, dy))(copy.start)


def finish_halo(copies, landed, field, rows, cols):
    low = (rows + 1) * PITCH

    def lay(way):
        if way == 0:
            field[pl.ds(low + 8, cols), :] = landed[0, 0:cols].astype(F32)
        elif way == 1:
            field[pl.ds(8, cols), :] = landed[1, 0:cols].astype(F32)
        elif way == 2:
            field[pl.ds(PITCH + 8 + cols, rows, stride=PITCH), :] = landed[2].astype(F32)
        elif way == 3:
            field[pl.ds(PITCH + 7, rows, stride=PITCH), :] = landed[3].astype(F32)
        elif way == 4:
            field[pl.ds(low + 8 + cols, 1), :] = landed[4, 0:16].astype(F32)[0:1]
        elif way == 5:
            field[pl.ds(low + 7, 1), :] = landed[5, 0:16].astype(F32)[0:1]
        elif way == 6:
            field[pl.ds(8 + cols, 1), :] = landed[6, 0:16].astype(F32)[15:16]
        else:
            field[pl.ds(7, 1), :] = landed[7, 0:16].astype(F32)[15:16]

    for way, ((dx, dy), copy) in enumerate(zip(DIRECTIONS, copies)):

        def arrive(way=way, copy=copy):
            copy.wait_recv()
            lay(way)

        pl.when(inside(-dx, -dy))(arrive)
        pl.when(inside(dx, dy))(copy.wait_send)


def clear_border(field, rows, cols):
    channels = field.shape[1]
    zeros = jnp.zeros((PITCH, channels), F32)
    field[pl.ds(0, PITCH), :] = zeros
    field[pl.ds((rows + 1) * PITCH, PITCH), :] = zeros
    for column in (7, 8 + cols):
        field[pl.ds(PITCH + column, rows, stride=PITCH), :] = jnp.zeros((rows, channels), F32)


def fill_borders(field, edges, sides, rows, cols):
    sides[0] = field[pl.ds(PITCH + 8, rows, stride=PITCH), :].astype(BF16)
    sides[1] = field[pl.ds(PITCH + 7 + cols, rows, stride=PITCH), :].astype(BF16)
    edges[0] = field[pl.ds(PITCH + 8, cols), :].astype(BF16)
    edges[1] = field[pl.ds(rows * PITCH + 8, cols), :].astype(BF16)


def spread_columns(field, wide, rows, cols):
    channels = field.shape[1]

    def row(x, carry):
        base = pl.multiple_of(x * PITCH, 8)
        at = pl.ds(pl.multiple_of(x * cols, cols), cols)
        for shift in range(3):
            wide[at, pl.ds(shift * channels, channels)] = field[
                pl.ds(base + 7 + shift, cols), :
            ].astype(BF16)
        return carry

    lax.fori_loop(0, rows + 2, row, 0)


def conv_rows(wide, weight, step, rows, cols):
    channels = weight.shape[1] // 2
    window = jnp.concatenate(
        [
            jnp.concatenate(
                [
                    wide[pl.ds(pl.multiple_of((step * rows + r + tap) * cols, cols), cols), :]
                    for r in range(0, rows, 2)
                ],
                axis=0,
            )
            for tap in range(4)
        ],
        axis=1,
    )
    both = dot(window, weight[...])
    return [
        both[(r // 2) * cols : (r // 2 + 1) * cols, (r % 2) * channels : (r % 2 + 1) * channels]
        for r in range(rows)
    ]


def double_weight(target, tap_weight, depth, channels):
    for tap in range(4):
        at = pl.ds(tap * depth, depth)
        for half in range(2):
            inner = tap - half
            lane = pl.ds(half * channels, channels)
            if 0 <= inner < 3:
                for third in range(3):
                    target[pl.ds(tap * depth + third * channels, channels), lane] = tap_weight(
                        inner, third
                    )
            else:
                target[at, lane] = jnp.zeros((depth, channels), BF16)


def position():
    count = lax.axis_size("bx") * lax.axis_size("by")
    return lax.axis_index("bx") * lax.axis_size("by") + lax.axis_index("by"), count


def greet_all(me, count):
    barrier = pltpu.get_barrier_semaphore()

    def greet(step, carry):
        pl.semaphore_signal(
            barrier, inc=1, device_id=place(lax.rem(me + step, count)), device_id_type=MESH
        )
        return carry

    lax.fori_loop(1, count, greet, 0)
    return barrier


def partner(me, pairs, step):
    return lax.rem(lax.div(me, 2) + lax.rem(step * STRIDE, pairs), pairs)


def source(me, pairs, step):
    return lax.rem(lax.div(me, 2) + pairs - lax.rem(step * STRIDE, pairs), pairs)


def send_pair(me, pairs, step, leaving, landing, sent, received):
    pair = partner(me, pairs, step)
    for side in range(2):
        tile = 2 * pair + side

        @pl.when(tile != me)
        def _(side=side, tile=tile):
            pltpu.make_async_remote_copy(
                src_ref=leaving.at[2 * step + side],
                dst_ref=landing.at[2 * step + lax.rem(me, 2)],
                send_sem=sent,
                recv_sem=received.at[lax.div(step, GROUP)],
                device_id=place(tile),
                device_id_type=MESH,
            ).start()


def wait_group(group, landing, received):
    full = pl.ds(0, 2 * GROUP)
    less = pl.ds(0, 2 * GROUP - 1)

    @pl.when(group == 0)
    def _():
        pltpu.make_async_copy(landing.at[less], landing.at[less], received.at[0]).wait()

    @pl.when(group > 0)
    def _():
        pltpu.make_async_copy(landing.at[full], landing.at[full], received.at[group]).wait()


def wait_sent(leaving, sent):
    others = pl.ds(0, leaving.shape[0] - 1)
    pltpu.make_async_copy(leaving.at[others], leaving.at[others], sent).wait()


def lift_kernel(
    counts, features, logits, ctx_weight, pixels, bins, cells_in, weight, proj, code_grad,
    lifted, slot_code, slot_weight, prob_out, ctx_out, weight_two, back_two, proj_two, slopes_in,
    cells_two, starts, point_code, outgoing, arrived, pooled, hot_cells, folded,
    local_sem, send_sem, recv_sem,
):
    me, count = position()
    pairs = count // 2
    my_side = lax.rem(me, 2)
    capacity = cells_in.shape[1]
    channels = weight.shape[1]
    bin_count, pix_count = logits.shape
    code_dims = proj.shape[1]
    all_cells = lifted.shape[0]
    cols = code_grad.shape[1]
    rows = all_cells // cols
    depth = 3 * channels
    barrier = greet_all(me, count)

    context = dot(features[...], ctx_weight[...]).astype(BF16)
    ctx_pair = jnp.concatenate([context, context], axis=0)
    raw = logits[...]
    shifted = jnp.exp(raw - jnp.max(raw, axis=0, keepdims=True))
    prob = shifted / jnp.sum(shifted, axis=0, keepdims=True)
    prob_out[...] = prob
    ctx_out[...] = context
    prob_pair = jnp.concatenate(halves(prob), axis=1)
    point_code[...] = pixels[...] * bin_count + bins[...]
    last_row = pixels.shape[0] - 1

    def start_of(tile, begin):
        starts[tile] = begin
        return begin + counts[0, tile]

    lax.fori_loop(0, count, start_of, 0)
    lane = lane_iota(1)
    pix_row = row_iota(pix_count)
    bin_row = row_iota(bin_count)

    def codes_of(pair):
        sides_codes = []
        for side in range(2):
            tile = 2 * pair + side
            begin = starts[tile]
            offset = jnp.bitwise_and(begin, LANES - 1)
            row = jnp.right_shift(begin, 7)
            here = point_code[pl.ds(jnp.minimum(row, last_row), 1), :]
            after = point_code[pl.ds(jnp.minimum(row + 1, last_row), 1), :]
            turned = pltpu.roll(
                jnp.where(lane >= offset, here, after),
                jnp.bitwise_and(side * capacity + LANES - offset, LANES - 1),
                axis=1,
            )
            sides_codes.append(jnp.where(lane - side * capacity < counts[0, tile], turned, -1))
        return jnp.where(lane < capacity, sides_codes[0], sides_codes[1])

    pl.semaphore_wait(barrier, count - 1)
    unroll = 4

    def lift(step, carry):
        for part in range(unroll):
            turn = step * unroll + part
            code = codes_of(partner(me, pairs, turn))
            slot_code[pl.ds(turn, 1), :] = code
            hot = jnp.right_shift(code, 6) == pix_row
            hot_b = jnp.where(hot, 1.0, 0.0).astype(BF16)
            picked = dot(prob_pair, jnp.concatenate([hot_b, hot_b], axis=0))
            chosen = jnp.bitwise_and(code, bin_count - 1) == bin_row
            point_weight = jnp.sum(jnp.where(chosen, picked, 0.0), axis=0, keepdims=True)
            slot_weight[pl.ds(turn, 1), :] = point_weight
            spread = jnp.concatenate(halves(jnp.where(hot, point_weight, 0.0)), axis=0)
            value = dot(spread, ctx_pair, TN).astype(BF16)
            outgoing[pl.ds(2 * turn, 2)] = value.reshape(2, capacity, channels)
        for part in range(unroll):
            send_pair(me, pairs, step * unroll + part, outgoing, arrived, send_sem, recv_sem)
        return carry

    lax.fori_loop(0, pairs // unroll, lift, 0)
    own = pltpu.make_async_copy(outgoing.at[my_side], arrived.at[my_side], local_sem)
    own.start()

    double_weight(
        weight_two,
        lambda tap, third: weight[pl.ds(tap * depth + third * channels, channels), :],
        depth,
        channels,
    )
    double_weight(
        back_two,
        lambda tap, third: weight[pl.ds((2 - tap) * depth + (2 - third) * channels, channels), :]
        .astype(F32)
        .T.astype(BF16),
        depth,
        channels,
    )
    proj_rows = dot(
        proj[...], jnp.where(row_iota(channels) == lane_iota(channels), 1.0, 0.0).astype(BF16), TN
    )
    proj_two[...] = jnp.zeros(proj_two.shape, F32)
    proj_two[0:code_dims] = proj_rows
    proj_two[8 : 8 + code_dims] = proj_rows
    slopes_in[...] = jnp.zeros(slopes_in.shape, F32)

    def take_slopes(step, carry):
        two = [code_grad[pl.ds(2 * step + r, code_dims, stride=rows), :] for r in range(2)]
        at = pl.ds(pl.multiple_of(step * 2 * cols, 2 * cols), 2 * cols)
        slopes_in[0:code_dims, at] = jnp.concatenate(two, axis=1)
        return carry

    lax.fori_loop(0, rows // 2, take_slopes, 0)
    pooled[...] = jnp.zeros(pooled.shape, F32)
    cells_two[...] = jnp.concatenate(
        [cells_in[pl.ds(side, pairs, stride=2), :] for side in range(2)], axis=1
    )
    run = all_cells // FOLD
    run_shift = run.bit_length() - 1
    run_row = row_iota(run)
    own.wait()

    def pool(group, carry):
        wait_group(group, arrived, recv_sem)
        for part in range(GROUP):
            turn = group * GROUP + part
            cell = cells_two[pl.ds(source(me, pairs, turn), 1), :]
            at = pl.ds(part * LANES, LANES)
            hot_cells[:, at] = jnp.where(
                jnp.bitwise_and(cell, run - 1) == run_row, 1.0, 0.0
            ).astype(BF16)
            which = jnp.broadcast_to(jnp.right_shift(cell, run_shift), (LANES, LANES)).T
            value = arrived[pl.ds(2 * turn, 2)].reshape(2 * capacity, channels).astype(F32)
            for fold in range(FOLD):
                folded[at, pl.ds(fold * channels, channels)] = jnp.where(
                    which == fold, value, 0.0
                ).astype(BF16)
        pooled[...] += dot(hot_cells[...], folded[...])
        return carry

    lax.fori_loop(0, pairs // GROUP, pool, 0)
    for fold in range(FOLD):
        lifted[pl.ds(fold * run, run), :] = pooled[:, pl.ds(fold * channels, channels)].astype(BF16)
    wait_sent(outgoing, send_sem)


def tile_kernel(
    levels, lifted, slot_code, slot_weight, prob_in, ctx_in, weight_two, back_two, proj_two_in,
    slopes_in, ctx_weight, cells_in,
    codes_out, logit_out, feature_out, sums,
    cells, returning, back, field, wide, wide_grad, lift_grad, sides, edges, landed, stage,
    parts, gathered, codes, flipped, prob_sum, ctx_sum,
    local_sem, back_send, back_recv, halo_send, halo_recv,
    part_send, part_recv, sum_send, sum_recv,
):
    me, count = position()
    pairs = count // 2
    my_side = lax.rem(me, 2)
    capacity = cells.shape[1]
    channels = lifted.shape[1]
    bin_count, pix_count = prob_in.shape
    cols = edges.shape[1]
    rows = sides.shape[1]
    code_dims = codes_out.shape[0] // rows
    depth = 3 * channels
    owners = parts.shape[0]
    all_cells = rows * cols
    barrier = greet_all(me, count)
    to_smem = pltpu.make_async_copy(cells_in, cells, local_sem.at[0])
    to_smem.start()
    pix_row = row_iota(pix_count)
    bin_row = row_iota(bin_count)
    clear_border(field, rows, cols)

    def load_row(x, carry):
        field[pl.ds(pl.multiple_of((x + 1) * PITCH + 8, 8), cols), :] = lifted[
            pl.ds(pl.multiple_of(x * cols, cols), cols), :
        ].astype(F32)
        return carry

    lax.fori_loop(0, rows, load_row, 0)
    fill_borders(field, edges, sides, rows, cols)
    pl.semaphore_wait(barrier, count - 1)
    first = halo_copies(edges, sides, landed.at[0], halo_send.at[0], halo_recv.at[0])
    start_halo(first)
    finish_halo(first, landed.at[0], field, rows, cols)
    spread_columns(field, wide, rows, cols)

    half_levels = jnp.zeros((8, 1), F32)
    for q in range(code_dims):
        half_levels = half_levels + jnp.where(
            lax.broadcasted_iota(I32, (8, 1), 0) == q, (levels[q].astype(F32) - 1.0) * 0.5, 0.0
        )
    proj_two = proj_two_in[...].astype(BF16)
    block = ENCODE_ROWS * cols

    def encode(step, proj_sum):
        origin = pl.multiple_of(step * block, block)
        conv_out = jnp.concatenate(conv_rows(wide, weight_two, step, ENCODE_ROWS, cols), axis=0)
        inv_rms = lax.rsqrt(jnp.mean(conv_out * conv_out, axis=-1, keepdims=True) + epsilon)
        normed = conv_out * inv_rms
        gate = 0.5 + 0.5 * jnp.tanh(0.5 * normed)
        active = normed * gate
        hidden = active.astype(BF16)
        squash = jnp.tanh(dot(proj_two, hidden, NT)[:8])
        codes[:, pl.ds(origin, block)] = half_levels * squash
        slope = slopes_in[:, pl.ds(origin, block)] * half_levels * (1.0 - squash * squash)
        slope_high = slope.astype(BF16).astype(F32)
        slope_pair = jnp.concatenate([slope_high, slope - slope_high], axis=0).astype(BF16)
        proj_both = dot(slope_pair, hidden)
        hidden_grad = dot(slope_pair, proj_two, TN)
        norm_grad = hidden_grad * (gate + active * (1.0 - gate))
        mixed = jnp.mean(norm_grad * normed, axis=-1, keepdims=True)
        conv_grad = inv_rms * (norm_grad - normed * mixed)
        for r in range(ENCODE_ROWS):
            at = pl.multiple_of((step * ENCODE_ROWS + r + 1) * PITCH + 8, 8)
            field[pl.ds(at, cols), :] = conv_grad[r * cols : (r + 1) * cols]
        wide_grad[pl.ds(origin + cols, block), pl.ds(channels, channels)] = conv_grad.astype(BF16)
        return proj_sum + proj_both[:8] + proj_both[8:]

    proj_sum = lax.fori_loop(0, rows // ENCODE_ROWS, encode, jnp.zeros((8, channels), F32))
    fill_borders(field, edges, sides, rows, cols)
    second = halo_copies(edges, sides, landed.at[1], halo_send.at[1], halo_recv.at[1])
    start_halo(second)

    flipped[...] = jnp.zeros(flipped.shape, F32)

    def weight_grad(step, carry):
        origin = pl.multiple_of(step * SPAN, SPAN)
        grad_t = wide_grad[pl.ds(origin + cols, SPAN), pl.ds(channels, channels)].T
        for tap in range(3):
            flipped[:, pl.ds(tap * depth, depth)] += dot(
                grad_t, wide[pl.ds(origin + tap * cols, SPAN), :]
            )
        return carry

    lax.fori_loop(0, all_cells // SPAN, weight_grad, 0)
    for tap in range(9):
        parts[pl.ds(tap * (channels // SHARE), channels // SHARE)] = flipped[
            :, pl.ds(tap * channels, channels)
        ].T.reshape(channels // SHARE, SHARE, channels)
    parts[owners - 1] = jnp.concatenate([proj_sum, jnp.zeros((SHARE - 8, channels), F32)], axis=0)

    def share_of(device):
        return lax.rem(device * SHARE_STRIDE, count)

    def send_part(step, carry):
        target = lax.rem(me + step, count)
        share = share_of(target)

        @pl.when(share < owners)
        def _():
            pltpu.make_async_remote_copy(
                src_ref=parts.at[share],
                dst_ref=gathered.at[me],
                send_sem=part_send,
                recv_sem=part_recv,
                device_id=place(target),
                device_id_type=MESH,
            ).start()

        return carry

    lax.fori_loop(1, count, send_part, 0)

    finish_halo(second, landed.at[1], field, rows, cols)
    spread_columns(field, wide_grad, rows, cols)

    def conv_back(step, carry):
        for r, row in enumerate(conv_rows(wide_grad, back_two, step, BACK_ROWS, cols)):
            at = pl.multiple_of((step * BACK_ROWS + r) * cols, cols)
            lift_grad[pl.ds(at, cols), :] = row
        return carry

    lax.fori_loop(0, rows // BACK_ROWS, conv_back, 0)

    to_smem.wait()

    def send_back(turn, carry):
        pair = partner(me, pairs, turn)
        for side in range(2):
            for slot in range(capacity):
                stage[pl.ds(side * capacity + slot, 1), :] = lift_grad[
                    pl.ds(cells[2 * pair + side, slot], 1), :
                ]
        returning[pl.ds(2 * turn, 2)] = stage[...].astype(BF16).reshape(2, capacity, channels)
        send_pair(me, pairs, turn, returning, back, back_send, back_recv)
        return carry

    lax.fori_loop(0, pairs // 2, send_back, 0)
    own_back = pltpu.make_async_copy(returning.at[my_side], back.at[my_side], local_sem.at[1])
    own_back.start()

    mine = share_of(me)
    others = pl.ds(0, count - 1)
    rest = pl.ds(0, owners - 1)

    @pl.when(mine < owners)
    def _():
        pltpu.make_async_copy(gathered.at[others], gathered.at[others], part_recv).wait()
        gathered[me] = parts[mine]

        def add(sender, total):
            return total + gathered[sender]

        sums[mine] = lax.fori_loop(0, count, add, jnp.zeros((SHARE, channels), F32))

        def send_sum(step, carry):
            pltpu.make_async_remote_copy(
                src_ref=sums.at[mine],
                dst_ref=sums.at[mine],
                send_sem=sum_send,
                recv_sem=sum_recv,
                device_id=place(lax.rem(me + step, count)),
                device_id_type=MESH,
            ).start()
            return carry

        lax.fori_loop(1, count, send_sum, 0)

    lax.fori_loop(pairs // 2, pairs, send_back, 0)
    own_back.wait()

    context = ctx_in[...]
    prob = prob_in[...]
    prob_sum[...] = jnp.zeros(prob_sum.shape, F32)
    ctx_sum[...] = jnp.zeros(ctx_sum.shape, F32)

    def point_grads(group, carry):
        wait_group(group, back, back_recv)
        prob_grad, ctx_grad = prob_sum[...], ctx_sum[...]
        for part in range(GROUP):
            turn = group * GROUP + part
            met = lax.rem(pairs - turn, pairs)
            code = slot_code[pl.ds(met, 1), :]
            grad = back[pl.ds(2 * turn, 2)].reshape(2 * capacity, channels)
            hot = jnp.right_shift(code, 6) == pix_row
            hot_b = jnp.where(hot, 1.0, 0.0).astype(BF16)
            chosen = jnp.bitwise_and(code, bin_count - 1) == bin_row
            dots = jnp.sum(jnp.where(hot, dot(context, grad, NT), 0.0), axis=0, keepdims=True)
            by_bin = jnp.concatenate(halves(jnp.where(chosen, dots, 0.0)), axis=1)
            prob_grad = prob_grad + dot(by_bin, jnp.concatenate([hot_b, hot_b], axis=1), NT)
            spread = jnp.concatenate(
                halves(jnp.where(hot, slot_weight[pl.ds(met, 1), :], 0.0)), axis=1
            )
            ctx_grad = ctx_grad + dot(spread, jnp.concatenate([grad, grad], axis=0))
        prob_sum[...] = prob_grad
        ctx_sum[...] = ctx_grad
        return carry

    lax.fori_loop(0, pairs // GROUP, point_grads, 0)
    prob_grad, ctx_grad = prob_sum[...], ctx_sum[...]
    logit_out[...] = prob * (prob_grad - jnp.sum(prob * prob_grad, axis=0, keepdims=True))
    feature_out[...] = dot(ctx_grad.astype(BF16), ctx_weight[...], NT).astype(BF16)

    def put_codes(step, carry):
        two = codes[0:code_dims, pl.ds(pl.multiple_of(step * 2 * cols, 2 * cols), 2 * cols)]
        for r in range(2):
            codes_out[pl.ds(2 * step + r, code_dims, stride=rows), :] = two[
                :, r * cols : (r + 1) * cols
            ]
        return carry

    lax.fori_loop(0, rows // 2, put_codes, 0)

    @pl.when(mine < owners)
    def _():
        pltpu.make_async_copy(gathered.at[others], gathered.at[others], sum_send).wait()
        pltpu.make_async_copy(parts.at[rest], parts.at[rest], part_send).wait()
        pltpu.make_async_copy(sums.at[rest], sums.at[rest], sum_recv).wait()

    @pl.when(mine >= owners)
    def _():
        pltpu.make_async_copy(parts, parts, part_send).wait()
        pltpu.make_async_copy(sums, sums, sum_recv).wait()

    wait_sent(returning, back_send)


def per_device(
    features,
    depth_logits,
    ctx_weight,
    point_pixel,
    point_bin,
    segment_count,
    slot_cell,
    conv_weight,
    proj_weight,
    level_count,
    code_grad,
):
    _, count, capacity = slot_cell.shape
    code_dims, rows, cols = code_grad.shape
    bin_count, pix_count = depth_logits.shape
    feature_dims, channels = ctx_weight.shape
    pixels = point_pixel.reshape(-1, LANES)
    bins = point_bin.reshape(-1, LANES)
    all_cells = rows * cols
    owners = 9 * channels // SHARE + 1
    pairs = count // 2
    run = all_cells // FOLD
    vmem = pl.BlockSpec(memory_space=pltpu.VMEM)
    smem = pl.BlockSpec(memory_space=pltpu.SMEM)
    wide = pltpu.VMEM(((rows + 2) * cols, 3 * channels), BF16)
    blocks = pltpu.VMEM((count, capacity, channels), BF16)
    doubled = jax.ShapeDtypeStruct((12 * channels, 2 * channels), BF16)
    dma = pltpu.SemaphoreType.DMA
    cells = slot_cell[0]
    lifted, slot_code, slot_weight, prob, context, weight_two, back_two, proj_two, slopes = (
        pl.pallas_call(
            lift_kernel,
            out_shape=(
                jax.ShapeDtypeStruct((all_cells, channels), BF16),
                jax.ShapeDtypeStruct((pairs, LANES), I32),
                jax.ShapeDtypeStruct((pairs, LANES), F32),
                jax.ShapeDtypeStruct((bin_count, pix_count), F32),
                jax.ShapeDtypeStruct((pix_count, channels), BF16),
                doubled,
                doubled,
                jax.ShapeDtypeStruct((16, channels), F32),
                jax.ShapeDtypeStruct((8, all_cells), F32),
            ),
            in_specs=[smem] + [vmem] * 9,
            out_specs=(vmem,) * 9,
            scratch_shapes=[
                pltpu.VMEM((pairs, 2 * capacity), I32),
                pltpu.SMEM((count,), I32),
                pltpu.VMEM(pixels.shape, I32),
                blocks,
                blocks,
                pltpu.VMEM((run, FOLD * channels), F32),
                pltpu.VMEM((run, GROUP * LANES), BF16),
                pltpu.VMEM((GROUP * LANES, FOLD * channels), BF16),
                dma,
                dma,
                dma((pairs // GROUP,)),
            ],
            compiler_params=pltpu.CompilerParams(
                collective_id=0, has_side_effects=True, vmem_limit_bytes=VMEM_LIMIT
            ),
            name="lift",
        )(
            segment_count,
            features,
            depth_logits,
            ctx_weight,
            pixels,
            bins,
            cells,
            conv_weight.reshape(9 * channels, channels),
            proj_weight,
            code_grad.reshape(code_dims * rows, cols),
        )
    )
    codes, grad_logits, grad_features, sums = pl.pallas_call(
        tile_kernel,
        out_shape=(
            jax.ShapeDtypeStruct((code_dims * rows, cols), F32),
            jax.ShapeDtypeStruct((bin_count, pix_count), F32),
            jax.ShapeDtypeStruct((pix_count, feature_dims), BF16),
            jax.ShapeDtypeStruct((owners, SHARE, channels), F32),
        ),
        in_specs=[smem] + [vmem] * 10 + [pl.BlockSpec(memory_space=pl.ANY)],
        out_specs=(vmem,) * 4,
        scratch_shapes=[
            pltpu.SMEM((count, capacity), I32),
            blocks,
            blocks,
            pltpu.VMEM(((rows + 2) * PITCH, channels), F32),
            wide,
            wide,
            pltpu.VMEM((all_cells, channels), F32),
            pltpu.VMEM((2, rows, channels), BF16),
            pltpu.VMEM((2, cols, channels), BF16),
            pltpu.VMEM((2, 8, rows, channels), BF16),
            pltpu.VMEM((2 * capacity, channels), F32),
            pltpu.VMEM((owners, SHARE, channels), F32),
            pltpu.VMEM((count, SHARE, channels), F32),
            pltpu.VMEM((8, all_cells), F32),
            pltpu.VMEM((channels, 9 * channels), F32),
            pltpu.VMEM((bin_count, pix_count), F32),
            pltpu.VMEM((pix_count, channels), F32),
            dma((2,)),
            dma,
            dma((pairs // GROUP,)),
            dma((2, 8)),
            dma((2, 8)),
            dma,
            dma,
            dma,
            dma,
        ],
        compiler_params=pltpu.CompilerParams(
            collective_id=1, has_side_effects=True, vmem_limit_bytes=VMEM_LIMIT
        ),
        name="tile",
    )(
        level_count,
        lifted,
        slot_code,
        slot_weight,
        prob,
        context,
        weight_two,
        back_two,
        proj_two,
        slopes,
        ctx_weight,
        cells,
    )
    return (
        codes.reshape(code_grad.shape),
        grad_logits,
        grad_features,
        sums[:-1].reshape(conv_weight.shape),
        sums[-1, :code_dims].T,
    )


def solution(mesh):
    return jax.shard_map(
        per_device,
        mesh=mesh,
        in_specs=(
            P(("bx", "by"), None),
            P(None, ("bx", "by")),
            P(),
            P(("bx", "by")),
            P(("bx", "by")),
            P(("bx", "by"), None),
            P(("bx", "by"), None, None),
            P(),
            P(),
            P(),
            P(None, "bx", "by"),
        ),
        out_specs=(P(None, "bx", "by"), P(None, ("bx", "by")), P(("bx", "by"), None), P(), P()),
        check_vma=False,
    )
```

time: 596 us -> 160 us (0.27); the launches traced: 587 us -> 159 us
  local copies, waits for them, and re-layouts: 189 us -> 12.6 us
  Pallas kernels: 0 us -> 146 us
  matrix products: 104 us -> 0 us
  waiting for transfers between devices: 91.7 us -> 0 us
  other arithmetic: 70.8 us -> 0 us
  blocking collectives: 68.6 us -> 0 us
  starting transfers between devices: 48 us -> 0 us
  between operations: 15.2 us -> 0.65 us
    gather x7 -> x0, local copies, waits for them, and re-layouts: 171 us -> none  [the longest x2 50.8 us: slot_values(): point_weight = jnp.where(usable, depth_prob[depths, pixels], 0.0)]
    pallas_call x0 -> x2, Pallas kernels: none -> 146 us  [the longest x1 90.2 us: per_device(): pl.pallas_call(tile_kernel, out_shape=(jax.ShapeDtypeStruct((code_dims *...]
    dot_general x34 -> x0, matrix products: 104 us -> none  [the longest x18 65.6 us: plane_dot(): jnp.dot(window.reshape(rows * cols, depth), weight, preferred_element_typ...]
    psum x1 -> x0, blocking collectives: 68.6 us -> none  [per_device(): grad_conv, grad_proj = lax.psum((conv_part, proj_part), ('bx', 'by'))]
    psum x1 -> x0, waiting for transfers between devices: 62.9 us -> none  [per_device(): grad_conv, grad_proj = lax.psum((conv_part, proj_part), ('bx', 'by'))]
    scatter-add x1 -> x0, other arithmetic: 46.4 us -> none  [per_device(): jax.ops.segment_sum(arrived.reshape(-1, channels).astype(jnp.float32), ta...]
    all_to_all x2 -> x0, waiting for transfers between devices: 28.8 us -> none  [the longest x1 28.8 us: per_device(): lax.all_to_all(carried, ('bx', 'by'), split_axis=0, concat_axis=0, tiled=...]
    all_to_all x2 -> x0, starting transfers between devices: 24.7 us -> none  [the longest x1 13.2 us: per_device(): lax.all_to_all(cell_grads, ('bx', 'by'), split_axis=0, concat_axis=0, til...]
  transfers between devices with their start and end apart: 11 -> 0, of which waited for: 2 -> 0; matrix products, arithmetic and copies ran while one was open for 8% -> 0% of each run, Pallas kernels for 0% -> 0%
where the time goes in v2:
time: 160 us; the launch traced here: 159 us
  Pallas kernels  146 us (91%)
  local copies, waits for them, and re-layouts  12.6 us (8%)
    pallas_call x1, Pallas kernels, per_device(): pl.pallas_call(tile_kernel, out_shape=(jax.ShapeDtypeStruct((code_dims *...  90.2 us
    pallas_call x1, Pallas kernels, per_device(): pl.pallas_call(lift_kernel, out_shape=(jax.ShapeDtypeStruct((all_cells, c...  55.7 us
    unnamed x6, local copies, waits for them, and re-layouts  9.41 us

profile of v2, /device:TPU:1, one launch (start us, length us, event | category | flops | bytes accessed | tf_op | source)
XLA Modules:
  0.0 159.2 jit_solution(16738479461950987604)
XLA Ops:
  0.6 1.4 copy.18.proj
  2.0 1.5 copy.16
  3.5 1.8 %copy.17 = f32[6,128,64]{2,1,0:T(8,128)} copy(f32[6,128,64]{1,2,0:T(8,128)} %param.21) | data formatting | bytes 393216 | tf_op args[10]
  5.4 55.7 %lift.1 = (bf16[8192,128]{1,0:T(8,128)(2,1)}, s32[64,128]{1,0:T(8,128)}, f32[64,128]{1,0:T(8,128)}, f32[64,128]{1,0:T(8,128)}, bf16[128,128]{1,0:T(8,128)(2,1)},...) custom-call(s32[1,128]{1,0:T(1,128)} %counts.1, ...), custom_call_target="tpu_custom_call" | custom-call | tf_op jit(solution)/shard_map/lift/pallas_call | solution.py:661
  61.1 90.2 %tile.1 = (f32[768,64]{1,0:T(8,128)}, f32[64,128]{1,0:T(8,128)}, bf16[128,256]{1,0:T(8,128)(2,1)}, f32[73,16,128]{2,1,0:T(8,128)}) custom-call(s32[6]{0:T(128)} %levels.1, bf16[8192,128]{1,0:T(8,128)(2,1)} %get-tuple-element.18.lifted, s32[64,128]{1,0:T(8,128)} %get-tuple-element.19.slot_code, f32[64,128]{1,0:T(8,128)} %get-tuple-element.20.slot_weight, ...), custom_call_target="tpu_custom_call" | custom-call | tf_op jit(solution)/shard_map/tile/pallas_call | solution.py:706
  151.4 1.8 %copy.19 = f32[6,128,64]{1,2,0:T(8,128)} copy(f32[6,128,64]{2,1,0:T(8,128)} %bitcast.15) | data formatting | bytes 393216
  153.2 1.3 slice_bitcast_fusion
  154.5 1.9 %slice.6 = f32[72,16,128]{2,1,0:T(8,128)} slice(f32[73,16,128]{2,1,0:T(8,128)} %get-tuple-element.30), slice={[0:72], [0:16], [0:128]} | slice | bytes 1179648 | tf_op jit(solution)/shard_map/slice | solution.py:766
  156.4 1.4 copy.22
  157.8 1.5 copy.23

commit v3 on v2

--- a/solution.py
+++ b/solution.py
@@ -22,7 +22,6 @@
 BACK_ROWS = 64
 SPAN = 2048
 SHARE = 16
-SHARE_STRIDE = 45
 DIRECTIONS = ((-1, 0), (1, 0), (0, -1), (0, 1), (-1, -1), (-1, 1), (1, -1), (1, 1))
 
 
@@ -254,16 +253,16 @@
 def lift_kernel(
     counts, features, logits, ctx_weight, pixels, bins, cells_in, weight, proj, code_grad,
     lifted, slot_code, slot_weight, prob_out, ctx_out, weight_two, back_two, proj_two, slopes_in,
-    cells_two, starts, point_code, outgoing, arrived, pooled, hot_cells, folded,
+    cells_two, cells_v, slopes_v, starts, point_code, outgoing, arrived, pooled, hot_cells, folded,
     local_sem, send_sem, recv_sem,
 ):
     me, count = position()
     pairs = count // 2
     my_side = lax.rem(me, 2)
-    capacity = cells_in.shape[1]
+    capacity = cells_in.shape[0]
     channels = weight.shape[1]
     bin_count, pix_count = logits.shape
-    code_dims = proj.shape[1]
+    code_dims = proj.shape[0]
     all_cells = lifted.shape[0]
     cols = code_grad.shape[1]
     rows = all_cells // cols
@@ -271,13 +270,13 @@
     barrier = greet_all(me, count)
 
     context = dot(features[...], ctx_weight[...]).astype(BF16)
-    ctx_pair = jnp.concatenate([context, context], axis=0)
     raw = logits[...]
     shifted = jnp.exp(raw - jnp.max(raw, axis=0, keepdims=True))
     prob = shifted / jnp.sum(shifted, axis=0, keepdims=True)
     prob_out[...] = prob
     ctx_out[...] = context
     prob_pair = jnp.concatenate(halves(prob), axis=1)
+    ctx_pair = jnp.concatenate([context, context], axis=0)
     point_code[...] = pixels[...] * bin_count + bins[...]
     last_row = pixels.shape[0] - 1
 
@@ -307,28 +306,39 @@
             sides_codes.append(jnp.where(lane - side * capacity < counts[0, tile], turned, -1))
         return jnp.where(lane < capacity, sides_codes[0], sides_codes[1])
 
+    def find_codes(step, carry):
+        for part in range(GROUP):
+            turn = step * GROUP + part
+            slot_code[pl.ds(turn, 1), :] = codes_of(partner(me, pairs, turn))
+        return carry
+
+    lax.fori_loop(0, pairs // GROUP, find_codes, 0)
+
     pl.semaphore_wait(barrier, count - 1)
-    unroll = 4
 
     def lift(step, carry):
-        for part in range(unroll):
-            turn = step * unroll + part
-            code = codes_of(partner(me, pairs, turn))
-            slot_code[pl.ds(turn, 1), :] = code
-            hot = jnp.right_shift(code, 6) == pix_row
-            hot_b = jnp.where(hot, 1.0, 0.0).astype(BF16)
-            picked = dot(prob_pair, jnp.concatenate([hot_b, hot_b], axis=0))
-            chosen = jnp.bitwise_and(code, bin_count - 1) == bin_row
-            point_weight = jnp.sum(jnp.where(chosen, picked, 0.0), axis=0, keepdims=True)
-            slot_weight[pl.ds(turn, 1), :] = point_weight
-            spread = jnp.concatenate(halves(jnp.where(hot, point_weight, 0.0)), axis=0)
-            value = dot(spread, ctx_pair, TN).astype(BF16)
-            outgoing[pl.ds(2 * turn, 2)] = value.reshape(2, capacity, channels)
-        for part in range(unroll):
-            send_pair(me, pairs, step * unroll + part, outgoing, arrived, send_sem, recv_sem)
-        return carry
-
-    lax.fori_loop(0, pairs // unroll, lift, 0)
+        code = slot_code[pl.ds(pl.multiple_of(step * GROUP, GROUP), GROUP), :]
+        code = jnp.concatenate([code[part : part + 1] for part in range(GROUP)], axis=1)
+        wide_rows = lax.broadcasted_iota(I32, (pix_count, GROUP * LANES), 0)
+        hot = jnp.right_shift(code, 6) == wide_rows
+        hot_b = jnp.where(hot, 1.0, 0.0).astype(BF16)
+        picked = dot(prob_pair, jnp.concatenate([hot_b, hot_b], axis=0))
+        chosen = jnp.bitwise_and(code, bin_count - 1) == wide_rows[:bin_count]
+        point_weight = jnp.sum(jnp.where(chosen, picked, 0.0), axis=0, keepdims=True)
+        for part in range(GROUP):
+            slot_weight[pl.ds(step * GROUP + part, 1), :] = point_weight[
+                :, part * LANES : (part + 1) * LANES
+            ]
+        spread = jnp.concatenate(halves(jnp.where(hot, point_weight, 0.0)), axis=0)
+        value = dot(spread, ctx_pair, TN).astype(BF16)
+        outgoing[pl.ds(2 * GROUP * step, 2 * GROUP)] = value.reshape(
+            2 * GROUP, capacity, channels
+        )
+        for part in range(GROUP):
+            send_pair(me, pairs, step * GROUP + part, outgoing, arrived, send_sem, recv_sem)
+        return carry
+
+    lax.fori_loop(0, pairs // GROUP, lift, 0)
     own = pltpu.make_async_copy(outgoing.at[my_side], arrived.at[my_side], local_sem)
     own.start()
 
@@ -346,24 +356,25 @@
         depth,
         channels,
     )
-    proj_rows = dot(
-        proj[...], jnp.where(row_iota(channels) == lane_iota(channels), 1.0, 0.0).astype(BF16), TN
-    )
+    proj_rows = proj[...].astype(F32)
     proj_two[...] = jnp.zeros(proj_two.shape, F32)
     proj_two[0:code_dims] = proj_rows
     proj_two[8 : 8 + code_dims] = proj_rows
     slopes_in[...] = jnp.zeros(slopes_in.shape, F32)
+    for q in range(code_dims):
+        slopes_v[pl.ds(q * rows, rows), :] = code_grad[q].T
 
     def take_slopes(step, carry):
-        two = [code_grad[pl.ds(2 * step + r, code_dims, stride=rows), :] for r in range(2)]
+        two = [slopes_v[pl.ds(2 * step + r, code_dims, stride=rows), :] for r in range(2)]
         at = pl.ds(pl.multiple_of(step * 2 * cols, 2 * cols), 2 * cols)
         slopes_in[0:code_dims, at] = jnp.concatenate(two, axis=1)
         return carry
 
     lax.fori_loop(0, rows // 2, take_slopes, 0)
     pooled[...] = jnp.zeros(pooled.shape, F32)
+    cells_v[...] = cells_in[...].T
     cells_two[...] = jnp.concatenate(
-        [cells_in[pl.ds(side, pairs, stride=2), :] for side in range(2)], axis=1
+        [cells_v[pl.ds(side, pairs, stride=2), :] for side in range(2)], axis=1
     )
     run = all_cells // FOLD
     run_shift = run.bit_length() - 1
@@ -396,24 +407,25 @@
 
 def tile_kernel(
     levels, lifted, slot_code, slot_weight, prob_in, ctx_in, weight_two, back_two, proj_two_in,
-    slopes_in, ctx_weight, cells_in,
-    codes_out, logit_out, feature_out, sums,
+    slopes_in, cells_in,
+    codes, prob_sum, ctx_sum, sums,
     cells, returning, back, field, wide, wide_grad, lift_grad, sides, edges, landed, stage,
-    parts, gathered, codes, flipped, prob_sum, ctx_sum,
+    parts, paired, chip_sums, gathered, sum_size, flipped,
     local_sem, back_send, back_recv, halo_send, halo_recv,
-    part_send, part_recv, sum_send, sum_recv,
+    pair_send, pair_recv, part_send, part_recv, sum_send, sum_recv,
 ):
     me, count = position()
     pairs = count // 2
     my_side = lax.rem(me, 2)
-    capacity = cells.shape[1]
+    capacity = cells.shape[0]
     channels = lifted.shape[1]
     bin_count, pix_count = prob_in.shape
     cols = edges.shape[1]
     rows = sides.shape[1]
-    code_dims = codes_out.shape[0] // rows
+    code_dims = levels.shape[0]
     depth = 3 * channels
     owners = parts.shape[0]
+    full_shares = 9 * channels // SHARE
     all_cells = rows * cols
     barrier = greet_all(me, count)
     to_smem = pltpu.make_async_copy(cells_in, cells, local_sem.at[0])
@@ -489,32 +501,51 @@
         parts[pl.ds(tap * (channels // SHARE), channels // SHARE)] = flipped[
             :, pl.ds(tap * channels, channels)
         ].T.reshape(channels // SHARE, SHARE, channels)
-    parts[owners - 1] = jnp.concatenate([proj_sum, jnp.zeros((SHARE - 8, channels), F32)], axis=0)
-
-    def share_of(device):
-        return lax.rem(device * SHARE_STRIDE, count)
+    parts[full_shares] = jnp.concatenate(
+        [proj_sum, jnp.zeros((SHARE - 8, channels), F32)], axis=0
+    )
+    for spare in range(full_shares + 1, owners):
+        parts[spare] = jnp.zeros((SHARE, channels), F32)
+
+    chips, half = count // 2, owners // 2
+    bx, by, _, row_devices = grid_place()
+    core = lax.rem(bx, 2)
+    chip = lax.div(bx, 2) * row_devices + by
+    to_sibling = pltpu.make_async_remote_copy(
+        src_ref=parts.at[pl.ds((1 - core) * half, half)],
+        dst_ref=paired,
+        send_sem=pair_send,
+        recv_sem=pair_recv,
+        device_id=(bx + 1 - 2 * core, by),
+        device_id_type=MESH,
+    )
+    to_sibling.start()
+
+    def share_of(one):
+        return lax.rem(one * STRIDE, chips)
 
     def send_part(step, carry):
-        target = lax.rem(me + step, count)
+        target = lax.rem(chip + step, chips)
         share = share_of(target)
 
-        @pl.when(share < owners)
+        @pl.when(share < half)
         def _():
             pltpu.make_async_remote_copy(
-                src_ref=parts.at[share],
-                dst_ref=gathered.at[me],
+                src_ref=chip_sums.at[share],
+                dst_ref=gathered.at[chip],
                 send_sem=part_send,
                 recv_sem=part_recv,
-                device_id=place(target),
+                device_id=(2 * lax.div(target, row_devices) + core, lax.rem(target, row_devices)),
                 device_id_type=MESH,
             ).start()
 
         return carry
 
-    lax.fori_loop(1, count, send_part, 0)
-
     finish_halo(second, landed.at[1], field, rows, cols)
     spread_columns(field, wide_grad, rows, cols)
+    to_sibling.wait()
+    chip_sums[...] = (parts[pl.ds(core * half, half)] + paired[...]).astype(BF16)
+    lax.fori_loop(1, chips, send_part, 0)
 
     def conv_back(step, carry):
         for r, row in enumerate(conv_rows(wide_grad, back_two, step, BACK_ROWS, cols)):
@@ -531,48 +562,52 @@
         for side in range(2):
             for slot in range(capacity):
                 stage[pl.ds(side * capacity + slot, 1), :] = lift_grad[
-                    pl.ds(cells[2 * pair + side, slot], 1), :
+                    pl.ds(cells[slot, 2 * pair + side], 1), :
                 ]
         returning[pl.ds(2 * turn, 2)] = stage[...].astype(BF16).reshape(2, capacity, channels)
         send_pair(me, pairs, turn, returning, back, back_send, back_recv)
         return carry
 
-    lax.fori_loop(0, pairs // 2, send_back, 0)
+    share = share_of(chip)
+    mine = core * half + share
+    others = pl.ds(0, chips - 1)
+    rest = pl.ds(0, half - 1)
+
+    def sum_parts():
+        @pl.when(share < half)
+        def _():
+            pltpu.make_async_copy(gathered.at[others], gathered.at[others], part_recv).wait()
+            gathered[chip] = chip_sums[share]
+
+            def add(sender, total):
+                return total + gathered[sender].astype(F32)
+
+            sums[mine] = lax.fori_loop(0, chips, add, jnp.zeros((SHARE, channels), F32)).astype(
+                BF16
+            )
+
+            def send_sum(step, carry):
+                pltpu.make_async_remote_copy(
+                    src_ref=sums.at[mine],
+                    dst_ref=sums.at[mine],
+                    send_sem=sum_send,
+                    recv_sem=sum_recv,
+                    device_id=place(lax.rem(me + step, count)),
+                    device_id_type=MESH,
+                ).start()
+                return carry
+
+            lax.fori_loop(1, count, send_sum, 0)
+
+    early = pairs // 8
+    lax.fori_loop(0, early, send_back, 0)
+    sum_parts()
+    lax.fori_loop(early, pairs, send_back, 0)
     own_back = pltpu.make_async_copy(returning.at[my_side], back.at[my_side], local_sem.at[1])
     own_back.start()
-
-    mine = share_of(me)
-    others = pl.ds(0, count - 1)
-    rest = pl.ds(0, owners - 1)
-
-    @pl.when(mine < owners)
-    def _():
-        pltpu.make_async_copy(gathered.at[others], gathered.at[others], part_recv).wait()
-        gathered[me] = parts[mine]
-
-        def add(sender, total):
-            return total + gathered[sender]
-
-        sums[mine] = lax.fori_loop(0, count, add, jnp.zeros((SHARE, channels), F32))
-
-        def send_sum(step, carry):
-            pltpu.make_async_remote_copy(
-                src_ref=sums.at[mine],
-                dst_ref=sums.at[mine],
-                send_sem=sum_send,
-                recv_sem=sum_recv,
-                device_id=place(lax.rem(me + step, count)),
-                device_id_type=MESH,
-            ).start()
-            return carry
-
-        lax.fori_loop(1, count, send_sum, 0)
-
-    lax.fori_loop(pairs // 2, pairs, send_back, 0)
     own_back.wait()
 
     context = ctx_in[...]
-    prob = prob_in[...]
     prob_sum[...] = jnp.zeros(prob_sum.shape, F32)
     ctx_sum[...] = jnp.zeros(ctx_sum.shape, F32)
 
@@ -590,41 +625,53 @@
             dots = jnp.sum(jnp.where(hot, dot(context, grad, NT), 0.0), axis=0, keepdims=True)
             by_bin = jnp.concatenate(halves(jnp.where(chosen, dots, 0.0)), axis=1)
             prob_grad = prob_grad + dot(by_bin, jnp.concatenate([hot_b, hot_b], axis=1), NT)
-            spread = jnp.concatenate(
-                halves(jnp.where(hot, slot_weight[pl.ds(met, 1), :], 0.0)), axis=1
-            )
-            ctx_grad = ctx_grad + dot(spread, jnp.concatenate([grad, grad], axis=0))
+            spread = jnp.where(hot, slot_weight[pl.ds(met, 1), :], 0.0).astype(BF16)
+            ctx_grad = ctx_grad + dot(spread, grad)
         prob_sum[...] = prob_grad
         ctx_sum[...] = ctx_grad
         return carry
 
     lax.fori_loop(0, pairs // GROUP, point_grads, 0)
-    prob_grad, ctx_grad = prob_sum[...], ctx_sum[...]
-    logit_out[...] = prob * (prob_grad - jnp.sum(prob * prob_grad, axis=0, keepdims=True))
-    feature_out[...] = dot(ctx_grad.astype(BF16), ctx_weight[...], NT).astype(BF16)
+    @pl.when(share < half)
+    def _():
+        sent_sums = sum_size.at[pl.ds(0, count - 1)]
+        pltpu.make_async_copy(sent_sums, sent_sums, sum_send).wait()
+        pltpu.make_async_copy(chip_sums.at[rest], chip_sums.at[rest], part_send).wait()
+        less = pl.ds(0, owners - 1)
+        pltpu.make_async_copy(sums.at[less], sums.at[less], sum_recv).wait()
+
+    @pl.when(share >= half)
+    def _():
+        pltpu.make_async_copy(chip_sums, chip_sums, part_send).wait()
+        pltpu.make_async_copy(sums, sums, sum_recv).wait()
+
+    wait_sent(returning, back_send)
+
+
+def finish_kernel(
+    codes, prob, prob_grad, ctx_grad, sums, ctx_weight,
+    codes_out, logit_out, feature_out, conv_out, proj_out,
+    by_row,
+):
+    code_dims, cols, rows = codes_out.shape
 
     def put_codes(step, carry):
         two = codes[0:code_dims, pl.ds(pl.multiple_of(step * 2 * cols, 2 * cols), 2 * cols)]
         for r in range(2):
-            codes_out[pl.ds(2 * step + r, code_dims, stride=rows), :] = two[
+            by_row[pl.ds(2 * step + r, code_dims, stride=rows), :] = two[
                 :, r * cols : (r + 1) * cols
             ]
         return carry
 
-    lax.fori_loop(0, rows // 2, put_codes, 0)
-
-    @pl.when(mine < owners)
-    def _():
-        pltpu.make_async_copy(gathered.at[others], gathered.at[others], sum_send).wait()
-        pltpu.make_async_copy(parts.at[rest], parts.at[rest], part_send).wait()
-        pltpu.make_async_copy(sums.at[rest], sums.at[rest], sum_recv).wait()
-
-    @pl.when(mine >= owners)
-    def _():
-        pltpu.make_async_copy(parts, parts, part_send).wait()
-        pltpu.make_async_copy(sums, sums, sum_recv).wait()
-
-    wait_sent(returning, back_send)
+    lax.fori_loop(0, rows // 2, put_codes, 0, unroll=4)
+    for q in range(code_dims):
+        codes_out[q] = by_row[pl.ds(q * rows, rows), :].T
+    chance, grad = prob[...], prob_grad[...]
+    logit_out[...] = chance * (grad - jnp.sum(chance * grad, axis=0, keepdims=True))
+    feature_out[...] = dot(ctx_grad[...].astype(BF16), ctx_weight[...], NT).astype(BF16)
+    for share in range(conv_out.shape[0] // SHARE):
+        conv_out[pl.ds(share * SHARE, SHARE), :] = sums[share].astype(F32)
+    proj_out[...] = sums[conv_out.shape[0] // SHARE].astype(F32)[0:code_dims]
 
 
 def per_device(
@@ -647,7 +694,7 @@
     pixels = point_pixel.reshape(-1, LANES)
     bins = point_bin.reshape(-1, LANES)
     all_cells = rows * cols
-    owners = 9 * channels // SHARE + 1
+    owners = (9 * channels // SHARE + 2) // 2 * 2
     pairs = count // 2
     run = all_cells // FOLD
     vmem = pl.BlockSpec(memory_space=pltpu.VMEM)
@@ -656,7 +703,7 @@
     blocks = pltpu.VMEM((count, capacity, channels), BF16)
     doubled = jax.ShapeDtypeStruct((12 * channels, 2 * channels), BF16)
     dma = pltpu.SemaphoreType.DMA
-    cells = slot_cell[0]
+    cells = slot_cell[0].T
     lifted, slot_code, slot_weight, prob, context, weight_two, back_two, proj_two, slopes = (
         pl.pallas_call(
             lift_kernel,
@@ -675,6 +722,8 @@
             out_specs=(vmem,) * 9,
             scratch_shapes=[
                 pltpu.VMEM((pairs, 2 * capacity), I32),
+                pltpu.VMEM((count, capacity), I32),
+                pltpu.VMEM((code_dims * rows, cols), F32),
                 pltpu.SMEM((count,), I32),
                 pltpu.VMEM(pixels.shape, I32),
                 blocks,
@@ -699,22 +748,22 @@
             bins,
             cells,
             conv_weight.reshape(9 * channels, channels),
-            proj_weight,
-            code_grad.reshape(code_dims * rows, cols),
+            proj_weight.T,
+            code_grad.transpose(0, 2, 1),
         )
     )
-    codes, grad_logits, grad_features, sums = pl.pallas_call(
+    codes, prob_grad, ctx_grad, sums = pl.pallas_call(
         tile_kernel,
         out_shape=(
-            jax.ShapeDtypeStruct((code_dims * rows, cols), F32),
+            jax.ShapeDtypeStruct((8, all_cells), F32),
             jax.ShapeDtypeStruct((bin_count, pix_count), F32),
-            jax.ShapeDtypeStruct((pix_count, feature_dims), BF16),
-            jax.ShapeDtypeStruct((owners, SHARE, channels), F32),
+            jax.ShapeDtypeStruct((pix_count, channels), F32),
+            jax.ShapeDtypeStruct((owners, SHARE, channels), BF16),
         ),
-        in_specs=[smem] + [vmem] * 10 + [pl.BlockSpec(memory_space=pl.ANY)],
+        in_specs=[smem] + [vmem] * 9 + [pl.BlockSpec(memory_space=pl.ANY)],
         out_specs=(vmem,) * 4,
         scratch_shapes=[
-            pltpu.SMEM((count, capacity), I32),
+            pltpu.SMEM((capacity, count), I32),
             blocks,
             blocks,
             pltpu.VMEM(((rows + 2) * PITCH, channels), F32),
@@ -726,16 +775,18 @@
             pltpu.VMEM((2, 8, rows, channels), BF16),
             pltpu.VMEM((2 * capacity, channels), F32),
             pltpu.VMEM((owners, SHARE, channels), F32),
-            pltpu.VMEM((count, SHARE, channels), F32),
-            pltpu.VMEM((8, all_cells), F32),
+            pltpu.VMEM((owners // 2, SHARE, channels), F32),
+            pltpu.VMEM((owners // 2, SHARE, channels), BF16),
+            pltpu.VMEM((count // 2, SHARE, channels), BF16),
+            pltpu.VMEM((count, SHARE, channels), BF16),
             pltpu.VMEM((channels, 9 * channels), F32),
-            pltpu.VMEM((bin_count, pix_count), F32),
-            pltpu.VMEM((pix_count, channels), F32),
             dma((2,)),
             dma,
             dma((pairs // GROUP,)),
             dma((2, 8)),
             dma((2, 8)),
+            dma,
+            dma,
             dma,
             dma,
             dma,
@@ -756,15 +807,29 @@
         back_two,
         proj_two,
         slopes,
-        ctx_weight,
         cells,
     )
+    codes_out, grad_logits, grad_features, grad_conv, grad_proj = pl.pallas_call(
+        finish_kernel,
+        out_shape=(
+            jax.ShapeDtypeStruct((code_dims, cols, rows), F32),
+            jax.ShapeDtypeStruct((bin_count, pix_count), F32),
+            jax.ShapeDtypeStruct((pix_count, feature_dims), BF16),
+            jax.ShapeDtypeStruct((9 * channels, channels), F32),
+            jax.ShapeDtypeStruct((code_dims, channels), F32),
+        ),
+        in_specs=[vmem] * 6,
+        out_specs=(vmem,) * 5,
+        scratch_shapes=[pltpu.VMEM((code_dims * rows, cols), F32)],
+        compiler_params=pltpu.CompilerParams(vmem_limit_bytes=VMEM_LIMIT),
+        name="finish",
+    )(codes, prob, prob_grad, ctx_grad, sums, ctx_weight)
     return (
-        codes.reshape(code_grad.shape),
+        codes_out.transpose(0, 2, 1),
         grad_logits,
         grad_features,
-        sums[:-1].reshape(conv_weight.shape),
-        sums[-1, :code_dims].T,
+        grad_conv.reshape(conv_weight.shape),
+        grad_proj.T,
     )
 
 

time: 160 us -> 125 us (0.78)
  Pallas kernels: 146 us -> 124 us
  local copies, waits for them, and re-layouts: 12.6 us -> 0 us
    pallas_call x1 -> x2, Pallas kernels: 90.2 us -> 75.4 us  [the longest x1 72.1 us: per_device(): pl.pallas_call(tile_kernel, out_shape=(jax.ShapeDtypeStruct((8, all_cells...]
    unnamed x6 -> x0, local copies, waits for them, and re-layouts: 9.41 us -> none
    pallas_call x1, Pallas kernels: 55.7 us -> 48.4 us  [per_device(): pl.pallas_call(lift_kernel, out_shape=(jax.ShapeDtypeStruct((all_cells, c...]
    slice x1 -> x0, local copies, waits for them, and re-layouts: 1.92 us -> none  [per_device(): sums[:-1].reshape(conv_weight.shape)]
where the time goes in v3:
time: 125 us
  Pallas kernels  124 us (99%)
    pallas_call x1, Pallas kernels, per_device(): pl.pallas_call(tile_kernel, out_shape=(jax.ShapeDtypeStruct((8, all_cells...  72.1 us
    pallas_call x1, Pallas kernels, per_device(): pl.pallas_call(lift_kernel, out_shape=(jax.ShapeDtypeStruct((all_cells, c...  48.4 us
    pallas_call x1, Pallas kernels, per_device(): pl.pallas_call(finish_kernel, out_shape=(jax.ShapeDtypeStruct((code_dims,...  3.36 us

profile of v3, /device:TPU:1, one launch (start us, length us, event | category | flops | bytes accessed | tf_op | source)
XLA Modules:
  0.0 124.5 jit_solution(11617378295401279624)
XLA Ops:
  0.6 48.4 %lift.1 = (bf16[8192,128]{1,0:T(8,128)(2,1)}, s32[64,128]{1,0:T(8,128)}, f32[64,128]{1,0:T(8,128)}, f32[64,128]{1,0:T(8,128)}, bf16[128,128]{1,0:T(8,128)(2,1)},...) custom-call(s32[1,128]{1,0:T(1,128)} %counts.1, ...), custom_call_target="tpu_custom_call" | custom-call | tf_op jit(solution)/shard_map/lift/pallas_call | solution.py:708
  49.1 72.1 %tile.1 = (f32[8,8192]{1,0:T(8,128)}, f32[64,128]{1,0:T(8,128)}, f32[128,128]{1,0:T(8,128)}, bf16[74,16,128]{2,1,0:T(8,128)(2,1)}) custom-call(s32[6]{0:T(128)} %levels.1, bf16[8192,128]{1,0:T(8,128)(2,1)} %get-tuple-element.23.lifted, s32[64,128]{1,0:T(8,128)} %get-tuple-element.24.slot_code, f32[64,128]{1,0:T(8,128)} %get-tuple-element.25.slot_weight, ...), custom_call_target="tpu_custom_call" | custom-call | tf_op jit(solution)/shard_map/tile/pallas_call | solution.py:755
  121.1 3.4 %finish.1 = (f32[6,64,128]{2,1,0:T(8,128)}, f32[64,128]{1,0:T(8,128)}, bf16[128,256]{1,0:T(8,128)(2,1)}, f32[1152,128]{1,0:T(8,128)}, f32[6,128]{1,0:T(8,128)}) custom-call(f32[8,8192]{1,0:T(8,128)} %get-tuple-element.32.codes, f32[64,128]{1,0:T(8,128)} %get-tuple-element.26.prob_in.prob, f32[64,128]{1,0:T(8,128)} %get-tuple-element.33.prob_grad, ...), custom_call_target="tpu_custom_call" | custom-call | tf_op jit(solution)/shard_map/finish/pallas_call | solution.py:812

commit v4 on v3

--- a/solution.py
+++ b/solution.py
@@ -15,7 +15,7 @@
 TN = (((0,), (0,)), ((), ()))
 LANES = 128
 PITCH = 80
-STRIDE = 45
+STRIDE = 37
 GROUP = 8
 FOLD = 8
 ENCODE_ROWS = 64
@@ -233,16 +233,9 @@
 
 
 def wait_group(group, landing, received):
-    full = pl.ds(0, 2 * GROUP)
-    less = pl.ds(0, 2 * GROUP - 1)
-
-    @pl.when(group == 0)
-    def _():
-        pltpu.make_async_copy(landing.at[less], landing.at[less], received.at[0]).wait()
-
-    @pl.when(group > 0)
-    def _():
-        pltpu.make_async_copy(landing.at[full], landing.at[full], received.at[group]).wait()
+    alone = isinstance(group, int) and group == 0
+    blocks = landing.at[pl.ds(0, 2 * GROUP - alone)]
+    pltpu.make_async_copy(blocks, blocks, received.at[group]).wait()
 
 
 def wait_sent(leaving, sent):
@@ -251,22 +244,17 @@
 
 
 def lift_kernel(
-    counts, features, logits, ctx_weight, pixels, bins, cells_in, weight, proj, code_grad,
-    lifted, slot_code, slot_weight, prob_out, ctx_out, weight_two, back_two, proj_two, slopes_in,
-    cells_two, cells_v, slopes_v, starts, point_code, outgoing, arrived, pooled, hot_cells, folded,
+    counts, features, logits, ctx_weight, pixels, bins, cells_in,
+    lifted, slot_code, slot_weight, prob_out, ctx_out,
+    cells_two, cells_v, starts, point_code, outgoing, arrived, pooled,
     local_sem, send_sem, recv_sem,
 ):
     me, count = position()
     pairs = count // 2
     my_side = lax.rem(me, 2)
     capacity = cells_in.shape[0]
-    channels = weight.shape[1]
+    all_cells, channels = lifted.shape
     bin_count, pix_count = logits.shape
-    code_dims = proj.shape[0]
-    all_cells = lifted.shape[0]
-    cols = code_grad.shape[1]
-    rows = all_cells // cols
-    depth = 3 * channels
     barrier = greet_all(me, count)
 
     context = dot(features[...], ctx_weight[...]).astype(BF16)
@@ -342,36 +330,6 @@
     own = pltpu.make_async_copy(outgoing.at[my_side], arrived.at[my_side], local_sem)
     own.start()
 
-    double_weight(
-        weight_two,
-        lambda tap, third: weight[pl.ds(tap * depth + third * channels, channels), :],
-        depth,
-        channels,
-    )
-    double_weight(
-        back_two,
-        lambda tap, third: weight[pl.ds((2 - tap) * depth + (2 - third) * channels, channels), :]
-        .astype(F32)
-        .T.astype(BF16),
-        depth,
-        channels,
-    )
-    proj_rows = proj[...].astype(F32)
-    proj_two[...] = jnp.zeros(proj_two.shape, F32)
-    proj_two[0:code_dims] = proj_rows
-    proj_two[8 : 8 + code_dims] = proj_rows
-    slopes_in[...] = jnp.zeros(slopes_in.shape, F32)
-    for q in range(code_dims):
-        slopes_v[pl.ds(q * rows, rows), :] = code_grad[q].T
-
-    def take_slopes(step, carry):
-        two = [slopes_v[pl.ds(2 * step + r, code_dims, stride=rows), :] for r in range(2)]
-        at = pl.ds(pl.multiple_of(step * 2 * cols, 2 * cols), 2 * cols)
-        slopes_in[0:code_dims, at] = jnp.concatenate(two, axis=1)
-        return carry
-
-    lax.fori_loop(0, rows // 2, take_slopes, 0)
-    pooled[...] = jnp.zeros(pooled.shape, F32)
     cells_v[...] = cells_in[...].T
     cells_two[...] = jnp.concatenate(
         [cells_v[pl.ds(side, pairs, stride=2), :] for side in range(2)], axis=1
@@ -381,22 +339,29 @@
     run_row = row_iota(run)
     own.wait()
 
+    pooled[...] = jnp.zeros(pooled.shape, F32)
+    wait_group(0, arrived, recv_sem)
+
     def pool(group, carry):
-        wait_group(group, arrived, recv_sem)
+        pl.when(group > 0)(lambda: wait_group(group, arrived, recv_sem))
+        hot_cells, folded = [], []
         for part in range(GROUP):
             turn = group * GROUP + part
             cell = cells_two[pl.ds(source(me, pairs, turn), 1), :]
-            at = pl.ds(part * LANES, LANES)
-            hot_cells[:, at] = jnp.where(
-                jnp.bitwise_and(cell, run - 1) == run_row, 1.0, 0.0
-            ).astype(BF16)
+            hot_cells.append(
+                jnp.where(jnp.bitwise_and(cell, run - 1) == run_row, 1.0, 0.0).astype(BF16)
+            )
             which = jnp.broadcast_to(jnp.right_shift(cell, run_shift), (LANES, LANES)).T
             value = arrived[pl.ds(2 * turn, 2)].reshape(2 * capacity, channels).astype(F32)
-            for fold in range(FOLD):
-                folded[at, pl.ds(fold * channels, channels)] = jnp.where(
-                    which == fold, value, 0.0
-                ).astype(BF16)
-        pooled[...] += dot(hot_cells[...], folded[...])
+            folded.append(
+                jnp.concatenate(
+                    [jnp.where(which == fold, value, 0.0).astype(BF16) for fold in range(FOLD)],
+                    axis=1,
+                )
+            )
+        pooled[...] += dot(
+            jnp.concatenate(hot_cells, axis=1), jnp.concatenate(folded, axis=0)
+        )
         return carry
 
     lax.fori_loop(0, pairs // GROUP, pool, 0)
@@ -406,20 +371,20 @@
 
 
 def tile_kernel(
-    levels, lifted, slot_code, slot_weight, prob_in, ctx_in, weight_two, back_two, proj_two_in,
-    slopes_in, cells_in,
-    codes, prob_sum, ctx_sum, sums,
+    levels, lifted, slot_code, slot_weight, ctx_in, weight, proj, code_grad, cells_in,
+    codes_out, prob_sum, ctx_sum, sums,
     cells, returning, back, field, wide, wide_grad, lift_grad, sides, edges, landed, stage,
-    parts, paired, chip_sums, gathered, sum_size, flipped,
+    parts, paired, chip_sums, gathered, flipped, weight_two, back_two, proj_two, slopes_in,
+    by_row, codes,
     local_sem, back_send, back_recv, halo_send, halo_recv,
-    pair_send, pair_recv, part_send, part_recv, sum_send, sum_recv,
+    pair_send, pair_recv, part_send, part_recv, sum_send, sum_recv, half_send, half_recv,
 ):
     me, count = position()
     pairs = count // 2
     my_side = lax.rem(me, 2)
     capacity = cells.shape[0]
     channels = lifted.shape[1]
-    bin_count, pix_count = prob_in.shape
+    bin_count, pix_count = prob_sum.shape
     cols = edges.shape[1]
     rows = sides.shape[1]
     code_dims = levels.shape[0]
@@ -445,6 +410,35 @@
     pl.semaphore_wait(barrier, count - 1)
     first = halo_copies(edges, sides, landed.at[0], halo_send.at[0], halo_recv.at[0])
     start_halo(first)
+    double_weight(
+        weight_two,
+        lambda tap, third: weight[pl.ds(tap * depth + third * channels, channels), :],
+        depth,
+        channels,
+    )
+    double_weight(
+        back_two,
+        lambda tap, third: weight[pl.ds((2 - tap) * depth + (2 - third) * channels, channels), :]
+        .astype(F32)
+        .T.astype(BF16),
+        depth,
+        channels,
+    )
+    proj_rows = proj[...].astype(F32)
+    proj_two[...] = jnp.zeros(proj_two.shape, F32)
+    proj_two[0:code_dims] = proj_rows
+    proj_two[8 : 8 + code_dims] = proj_rows
+    slopes_in[...] = jnp.zeros(slopes_in.shape, F32)
+    for q in range(code_dims):
+        by_row[pl.ds(q * rows, rows), :] = code_grad[q].T
+
+    def take_slopes(step, carry):
+        two = [by_row[pl.ds(2 * step + r, code_dims, stride=rows), :] for r in range(2)]
+        at = pl.ds(pl.multiple_of(step * 2 * cols, 2 * cols), 2 * cols)
+        slopes_in[0:code_dims, at] = jnp.concatenate(two, axis=1)
+        return carry
+
+    lax.fori_loop(0, rows // 2, take_slopes, 0)
     finish_halo(first, landed.at[0], field, rows, cols)
     spread_columns(field, wide, rows, cols)
 
@@ -453,7 +447,7 @@
         half_levels = half_levels + jnp.where(
             lax.broadcasted_iota(I32, (8, 1), 0) == q, (levels[q].astype(F32) - 1.0) * 0.5, 0.0
         )
-    proj_two = proj_two_in[...].astype(BF16)
+    proj_both_rows = proj_two[...].astype(BF16)
     block = ENCODE_ROWS * cols
 
     def encode(step, proj_sum):
@@ -464,13 +458,13 @@
         gate = 0.5 + 0.5 * jnp.tanh(0.5 * normed)
         active = normed * gate
         hidden = active.astype(BF16)
-        squash = jnp.tanh(dot(proj_two, hidden, NT)[:8])
+        squash = jnp.tanh(dot(proj_both_rows, hidden, NT)[:8])
         codes[:, pl.ds(origin, block)] = half_levels * squash
         slope = slopes_in[:, pl.ds(origin, block)] * half_levels * (1.0 - squash * squash)
         slope_high = slope.astype(BF16).astype(F32)
         slope_pair = jnp.concatenate([slope_high, slope - slope_high], axis=0).astype(BF16)
         proj_both = dot(slope_pair, hidden)
-        hidden_grad = dot(slope_pair, proj_two, TN)
+        hidden_grad = dot(slope_pair, proj_both_rows, TN)
         norm_grad = hidden_grad * (gate + active * (1.0 - gate))
         mixed = jnp.mean(norm_grad * normed, axis=-1, keepdims=True)
         conv_grad = inv_rms * (norm_grad - normed * mixed)
@@ -520,6 +514,18 @@
         device_id_type=MESH,
     )
     to_sibling.start()
+    my_half = sums.at[pl.ds(core * half, half)]
+    half_to_sibling = pltpu.make_async_remote_copy(
+        src_ref=my_half,
+        dst_ref=my_half,
+        send_sem=half_send,
+        recv_sem=half_recv,
+        device_id=(bx + 1 - 2 * core, by),
+        device_id_type=MESH,
+    )
+
+    def same_core(one):
+        return (2 * lax.div(one, row_devices) + core, lax.rem(one, row_devices))
 
     def share_of(one):
         return lax.rem(one * STRIDE, chips)
@@ -535,7 +541,7 @@
                 dst_ref=gathered.at[chip],
                 send_sem=part_send,
                 recv_sem=part_recv,
-                device_id=(2 * lax.div(target, row_devices) + core, lax.rem(target, row_devices)),
+                device_id=same_core(target),
                 device_id_type=MESH,
             ).start()
 
@@ -592,12 +598,12 @@
                     dst_ref=sums.at[mine],
                     send_sem=sum_send,
                     recv_sem=sum_recv,
-                    device_id=place(lax.rem(me + step, count)),
+                    device_id=same_core(lax.rem(chip + step, chips)),
                     device_id_type=MESH,
                 ).start()
                 return carry
 
-            lax.fori_loop(1, count, send_sum, 0)
+            lax.fori_loop(1, chips, send_sum, 0)
 
     early = pairs // 8
     lax.fori_loop(0, early, send_back, 0)
@@ -607,12 +613,28 @@
     own_back.start()
     own_back.wait()
 
+    def put_codes(step, carry):
+        two = codes[0:code_dims, pl.ds(pl.multiple_of(step * 2 * cols, 2 * cols), 2 * cols)]
+        for r in range(2):
+            by_row[pl.ds(2 * step + r, code_dims, stride=rows), :] = two[
+                :, r * cols : (r + 1) * cols
+            ]
+        return carry
+
+    lax.fori_loop(0, rows // 2, put_codes, 0)
+    for q in range(code_dims):
+        codes_out[q] = by_row[pl.ds(q * rows, rows), :].T
+
     context = ctx_in[...]
     prob_sum[...] = jnp.zeros(prob_sum.shape, F32)
     ctx_sum[...] = jnp.zeros(ctx_sum.shape, F32)
 
     def point_grads(group, carry):
         wait_group(group, back, back_recv)
+        add_points(group)
+        return carry
+
+    def add_points(group):
         prob_grad, ctx_grad = prob_sum[...], ctx_sum[...]
         for part in range(GROUP):
             turn = group * GROUP + part
@@ -629,43 +651,36 @@
             ctx_grad = ctx_grad + dot(spread, grad)
         prob_sum[...] = prob_grad
         ctx_sum[...] = ctx_grad
-        return carry
-
-    lax.fori_loop(0, pairs // GROUP, point_grads, 0)
+
+    wait_group(0, back, back_recv)
+    add_points(0)
+
+    late = pairs // GROUP - 2
+    lax.fori_loop(1, late, point_grads, 0)
+
     @pl.when(share < half)
     def _():
-        sent_sums = sum_size.at[pl.ds(0, count - 1)]
-        pltpu.make_async_copy(sent_sums, sent_sums, sum_send).wait()
+        pltpu.make_async_copy(gathered.at[others], gathered.at[others], sum_send).wait()
         pltpu.make_async_copy(chip_sums.at[rest], chip_sums.at[rest], part_send).wait()
-        less = pl.ds(0, owners - 1)
-        pltpu.make_async_copy(sums.at[less], sums.at[less], sum_recv).wait()
+        pltpu.make_async_copy(chip_sums.at[rest], chip_sums.at[rest], sum_recv).wait()
 
     @pl.when(share >= half)
     def _():
         pltpu.make_async_copy(chip_sums, chip_sums, part_send).wait()
-        pltpu.make_async_copy(sums, sums, sum_recv).wait()
-
+        pltpu.make_async_copy(chip_sums, chip_sums, sum_recv).wait()
+
+    half_to_sibling.start()
+    lax.fori_loop(late, pairs // GROUP, point_grads, 0)
+    half_to_sibling.wait()
     wait_sent(returning, back_send)
 
 
 def finish_kernel(
     codes, prob, prob_grad, ctx_grad, sums, ctx_weight,
     codes_out, logit_out, feature_out, conv_out, proj_out,
-    by_row,
 ):
-    code_dims, cols, rows = codes_out.shape
-
-    def put_codes(step, carry):
-        two = codes[0:code_dims, pl.ds(pl.multiple_of(step * 2 * cols, 2 * cols), 2 * cols)]
-        for r in range(2):
-            by_row[pl.ds(2 * step + r, code_dims, stride=rows), :] = two[
-                :, r * cols : (r + 1) * cols
-            ]
-        return carry
-
-    lax.fori_loop(0, rows // 2, put_codes, 0, unroll=4)
-    for q in range(code_dims):
-        codes_out[q] = by_row[pl.ds(q * rows, rows), :].T
+    code_dims = codes_out.shape[0]
+    codes_out[...] = codes[...]
     chance, grad = prob[...], prob_grad[...]
     logit_out[...] = chance * (grad - jnp.sum(chance * grad, axis=0, keepdims=True))
     feature_out[...] = dot(ctx_grad[...].astype(BF16), ctx_weight[...], NT).astype(BF16)
@@ -701,10 +716,11 @@
     smem = pl.BlockSpec(memory_space=pltpu.SMEM)
     wide = pltpu.VMEM(((rows + 2) * cols, 3 * channels), BF16)
     blocks = pltpu.VMEM((count, capacity, channels), BF16)
-    doubled = jax.ShapeDtypeStruct((12 * channels, 2 * channels), BF16)
+    doubled = pltpu.VMEM((12 * channels, 2 * channels), BF16)
+    weight = conv_weight.reshape(9 * channels, channels)
     dma = pltpu.SemaphoreType.DMA
     cells = slot_cell[0].T
-    lifted, slot_code, slot_weight, prob, context, weight_two, back_two, proj_two, slopes = (
+    lifted, slot_code, slot_weight, prob, context = (
         pl.pallas_call(
             lift_kernel,
             out_shape=(
@@ -713,24 +729,17 @@
                 jax.ShapeDtypeStruct((pairs, LANES), F32),
                 jax.ShapeDtypeStruct((bin_count, pix_count), F32),
                 jax.ShapeDtypeStruct((pix_count, channels), BF16),
-                doubled,
-                doubled,
-                jax.ShapeDtypeStruct((16, channels), F32),
-                jax.ShapeDtypeStruct((8, all_cells), F32),
             ),
-            in_specs=[smem] + [vmem] * 9,
-            out_specs=(vmem,) * 9,
+            in_specs=[smem] + [vmem] * 6,
+            out_specs=(vmem,) * 5,
             scratch_shapes=[
                 pltpu.VMEM((pairs, 2 * capacity), I32),
                 pltpu.VMEM((count, capacity), I32),
-                pltpu.VMEM((code_dims * rows, cols), F32),
                 pltpu.SMEM((count,), I32),
                 pltpu.VMEM(pixels.shape, I32),
                 blocks,
                 blocks,
                 pltpu.VMEM((run, FOLD * channels), F32),
-                pltpu.VMEM((run, GROUP * LANES), BF16),
-                pltpu.VMEM((GROUP * LANES, FOLD * channels), BF16),
                 dma,
                 dma,
                 dma((pairs // GROUP,)),
@@ -747,20 +756,17 @@
             pixels,
             bins,
             cells,
-            conv_weight.reshape(9 * channels, channels),
-            proj_weight.T,
-            code_grad.transpose(0, 2, 1),
         )
     )
     codes, prob_grad, ctx_grad, sums = pl.pallas_call(
         tile_kernel,
         out_shape=(
-            jax.ShapeDtypeStruct((8, all_cells), F32),
+            jax.ShapeDtypeStruct((code_dims, cols, rows), F32),
             jax.ShapeDtypeStruct((bin_count, pix_count), F32),
             jax.ShapeDtypeStruct((pix_count, channels), F32),
             jax.ShapeDtypeStruct((owners, SHARE, channels), BF16),
         ),
-        in_specs=[smem] + [vmem] * 9 + [pl.BlockSpec(memory_space=pl.ANY)],
+        in_specs=[smem] + [vmem] * 7 + [pl.BlockSpec(memory_space=pl.ANY)],
         out_specs=(vmem,) * 4,
         scratch_shapes=[
             pltpu.SMEM((capacity, count), I32),
@@ -778,13 +784,20 @@
             pltpu.VMEM((owners // 2, SHARE, channels), F32),
             pltpu.VMEM((owners // 2, SHARE, channels), BF16),
             pltpu.VMEM((count // 2, SHARE, channels), BF16),
-            pltpu.VMEM((count, SHARE, channels), BF16),
             pltpu.VMEM((channels, 9 * channels), F32),
+            doubled,
+            doubled,
+            pltpu.VMEM((16, channels), F32),
+            pltpu.VMEM((8, all_cells), F32),
+            pltpu.VMEM((code_dims * rows, cols), F32),
+            pltpu.VMEM((8, all_cells), F32),
             dma((2,)),
             dma,
             dma((pairs // GROUP,)),
             dma((2, 8)),
             dma((2, 8)),
+            dma,
+            dma,
             dma,
             dma,
             dma,
@@ -801,12 +814,10 @@
         lifted,
         slot_code,
         slot_weight,
-        prob,
         context,
-        weight_two,
-        back_two,
-        proj_two,
-        slopes,
+        weight,
+        proj_weight.T,
+        code_grad.transpose(0, 2, 1),
         cells,
     )
     codes_out, grad_logits, grad_features, grad_conv, grad_proj = pl.pallas_call(
@@ -820,7 +831,6 @@
         ),
         in_specs=[vmem] * 6,
         out_specs=(vmem,) * 5,
-        scratch_shapes=[pltpu.VMEM((code_dims * rows, cols), F32)],
         compiler_params=pltpu.CompilerParams(vmem_limit_bytes=VMEM_LIMIT),
         name="finish",
     )(codes, prob, prob_grad, ctx_grad, sums, ctx_weight)

time: 125 us -> 116 us (0.928)
  Pallas kernels: 124 us -> 116 us
    pallas_call x1, Pallas kernels: 72.1 us -> 67.8 us  [per_device(): pl.pallas_call(tile_kernel, out_shape=(jax.ShapeDtypeStruct((code_dims, c...]
    pallas_call x1, Pallas kernels: 48.4 us -> 45.6 us  [per_device(): pl.pallas_call(lift_kernel, out_shape=(jax.ShapeDtypeStruct((all_cells, c...]
where the time goes in v4:
time: 116 us
  Pallas kernels  116 us (100%)
    pallas_call x1, Pallas kernels, per_device(): pl.pallas_call(tile_kernel, out_shape=(jax.ShapeDtypeStruct((code_dims, c...  67.8 us
    pallas_call x1, Pallas kernels, per_device(): pl.pallas_call(lift_kernel, out_shape=(jax.ShapeDtypeStruct((all_cells, c...  45.6 us

profile of v4, /device:TPU:1, one launch (start us, length us, event | category | flops | bytes accessed | tf_op | source)
XLA Modules:
  0.0 116.2 jit_solution(15373118470899201160)
XLA Ops:
  0.6 45.6 %lift.1 = (bf16[8192,128]{1,0:T(8,128)(2,1)}, s32[64,128]{1,0:T(8,128)}, f32[64,128]{1,0:T(8,128)}, f32[64,128]{1,0:T(8,128)}, bf16[128,128]{1,0:T(8,128)(2,1)}) custom-call(s32[1,128]{1,0:T(1,128)} %counts.1, bf16[128,256]{1,0:T(8,128)(2,1)} %features.1, f32[64,128]{1,0:T(8,128)} %logits.1, bf16[256,128]{1,0:T(8,128)(2,1)} %ctx_weight.3, ...), custom_call_target="tpu_custom_call" | custom-call | tf_op jit(solution)/shard_map/lift/pallas_call | solution.py:724
  46.3 67.8 %tile.1 = (f32[6,64,128]{2,1,0:T(8,128)}, f32[64,128]{1,0:T(8,128)}, f32[128,128]{1,0:T(8,128)}, bf16[74,16,128]{2,1,0:T(8,128)(2,1)}) custom-call(s32[6]{0:T(128)} %levels.1, bf16[8192,128]{1,0:T(8,128)(2,1)} %get-tuple-element.19.lifted, s32[64,128]{1,0:T(8,128)} %get-tuple-element.20.slot_code, f32[64,128]{1,0:T(8,128)} %get-tuple-element.21.slot_weight, ...), custom_call_target="tpu_custom_call" | custom-call | tf_op jit(solution)/shard_map/tile/pallas_call | solution.py:761
  114.1 2.1 %finish.1 = (f32[6,64,128]{2,1,0:T(8,128)}, f32[64,128]{1,0:T(8,128)}, bf16[128,256]{1,0:T(8,128)(2,1)}, f32[1152,128]{1,0:T(8,128)}, f32[6,128]{1,0:T(8,128)}) custom-call(f32[6,64,128]{2,1,0:T(8,128)} %get-tuple-element.23.codes, f32[64,128]{1,0:T(8,128)} %get-tuple-element.24.prob, f32[64,128]{1,0:T(8,128)} %get-tuple-element.25.prob_grad, ...), custom_call_target="tpu_custom_call" | custom-call | tf_op jit(solution)/shard_map/finish/pallas_call | solution.py:823

commit v5 on v4

--- a/solution.py
+++ b/solution.py
@@ -15,7 +15,8 @@
 TN = (((0,), (0,)), ((), ()))
 LANES = 128
 PITCH = 80
-STRIDE = 37
+STRIDE = 11
+AHEAD = 4
 GROUP = 8
 FOLD = 8
 ENCODE_ROWS = 64
@@ -34,9 +35,17 @@
     return high, (value - high.astype(F32)).astype(BF16)
 
 
+def shared(index, size):
+    return jnp.bitwise_and(index, size - 1)
+
+
+def parted(index, size):
+    return jnp.right_shift(index, size.bit_length() - 1)
+
+
 def place(index):
     cols = lax.axis_size("by")
-    return (lax.div(index, cols), lax.rem(index, cols))
+    return (parted(index, cols), shared(index, cols))
 
 
 def grid_place():
@@ -149,7 +158,7 @@
             ].astype(BF16)
         return carry
 
-    lax.fori_loop(0, rows + 2, row, 0)
+    lax.fori_loop(0, rows + 2, row, 0, unroll=5)
 
 
 def conv_rows(wide, weight, step, rows, cols):
@@ -199,20 +208,23 @@
 
     def greet(step, carry):
         pl.semaphore_signal(
-            barrier, inc=1, device_id=place(lax.rem(me + step, count)), device_id_type=MESH
+            barrier, inc=1, device_id=place(shared(me + step, count)), device_id_type=MESH
         )
         return carry
 
-    lax.fori_loop(1, count, greet, 0)
+    even = 1 + (count - 1) // 8 * 8
+    lax.fori_loop(1, even, greet, 0, unroll=8)
+    for step in range(even, count):
+        greet(step, 0)
     return barrier
 
 
 def partner(me, pairs, step):
-    return lax.rem(lax.div(me, 2) + lax.rem(step * STRIDE, pairs), pairs)
+    return shared(parted(me, 2) + step * STRIDE, pairs)
 
 
 def source(me, pairs, step):
-    return lax.rem(lax.div(me, 2) + pairs - lax.rem(step * STRIDE, pairs), pairs)
+    return shared(parted(me, 2) + pairs * STRIDE - step * STRIDE, pairs)
 
 
 def send_pair(me, pairs, step, leaving, landing, sent, received):
@@ -224,9 +236,9 @@
         def _(side=side, tile=tile):
             pltpu.make_async_remote_copy(
                 src_ref=leaving.at[2 * step + side],
-                dst_ref=landing.at[2 * step + lax.rem(me, 2)],
+                dst_ref=landing.at[2 * step + shared(me, 2)],
                 send_sem=sent,
-                recv_sem=received.at[lax.div(step, GROUP)],
+                recv_sem=received.at[parted(step, GROUP)],
                 device_id=place(tile),
                 device_id_type=MESH,
             ).start()
@@ -251,7 +263,7 @@
 ):
     me, count = position()
     pairs = count // 2
-    my_side = lax.rem(me, 2)
+    my_side = shared(me, 2)
     capacity = cells_in.shape[0]
     all_cells, channels = lifted.shape
     bin_count, pix_count = logits.shape
@@ -272,7 +284,7 @@
         starts[tile] = begin
         return begin + counts[0, tile]
 
-    lax.fori_loop(0, count, start_of, 0)
+    lax.fori_loop(0, count, start_of, 0, unroll=8)
     lane = lane_iota(1)
     pix_row = row_iota(pix_count)
     bin_row = row_iota(bin_count)
@@ -294,19 +306,13 @@
             sides_codes.append(jnp.where(lane - side * capacity < counts[0, tile], turned, -1))
         return jnp.where(lane < capacity, sides_codes[0], sides_codes[1])
 
-    def find_codes(step, carry):
+    pl.semaphore_wait(barrier, count - 1)
+
+    def lift(step, carry):
+        found = [codes_of(partner(me, pairs, step * GROUP + part)) for part in range(GROUP)]
         for part in range(GROUP):
-            turn = step * GROUP + part
-            slot_code[pl.ds(turn, 1), :] = codes_of(partner(me, pairs, turn))
-        return carry
-
-    lax.fori_loop(0, pairs // GROUP, find_codes, 0)
-
-    pl.semaphore_wait(barrier, count - 1)
-
-    def lift(step, carry):
-        code = slot_code[pl.ds(pl.multiple_of(step * GROUP, GROUP), GROUP), :]
-        code = jnp.concatenate([code[part : part + 1] for part in range(GROUP)], axis=1)
+            slot_code[pl.ds(step * GROUP + part, 1), :] = found[part]
+        code = jnp.concatenate(found, axis=1)
         wide_rows = lax.broadcasted_iota(I32, (pix_count, GROUP * LANES), 0)
         hot = jnp.right_shift(code, 6) == wide_rows
         hot_b = jnp.where(hot, 1.0, 0.0).astype(BF16)
@@ -322,9 +328,15 @@
         outgoing[pl.ds(2 * GROUP * step, 2 * GROUP)] = value.reshape(
             2 * GROUP, capacity, channels
         )
-        for part in range(GROUP):
-            send_pair(me, pairs, step * GROUP + part, outgoing, arrived, send_sem, recv_sem)
-        return carry
+        pl.when(step < AHEAD)(lambda: send_group(step))
+        return carry
+
+    def send_group(step):
+        def send(turn, carry):
+            send_pair(me, pairs, turn, outgoing, arrived, send_sem, recv_sem)
+            return carry
+
+        lax.fori_loop(step * GROUP, (step + 1) * GROUP, send, 0)
 
     lax.fori_loop(0, pairs // GROUP, lift, 0)
     own = pltpu.make_async_copy(outgoing.at[my_side], arrived.at[my_side], local_sem)
@@ -343,6 +355,7 @@
     wait_group(0, arrived, recv_sem)
 
     def pool(group, carry):
+        pl.when(group + AHEAD < pairs // GROUP)(lambda: send_group(group + AHEAD))
         pl.when(group > 0)(lambda: wait_group(group, arrived, recv_sem))
         hot_cells, folded = [], []
         for part in range(GROUP):
@@ -371,9 +384,9 @@
 
 
 def tile_kernel(
-    levels, lifted, slot_code, slot_weight, ctx_in, weight, proj, code_grad, cells_in,
+    levels, lifted_in, slot_code, slot_weight, ctx_in, weight, proj, code_grad, cells_in,
     codes_out, prob_sum, ctx_sum, sums,
-    cells, returning, back, field, wide, wide_grad, lift_grad, sides, edges, landed, stage,
+    cells, lifted, returning, back, field, wide, wide_grad, lift_grad, sides, edges, landed, stage,
     parts, paired, chip_sums, gathered, flipped, weight_two, back_two, proj_two, slopes_in,
     by_row, codes,
     local_sem, back_send, back_recv, halo_send, halo_recv,
@@ -381,9 +394,11 @@
 ):
     me, count = position()
     pairs = count // 2
-    my_side = lax.rem(me, 2)
+    my_side = shared(me, 2)
     capacity = cells.shape[0]
     channels = lifted.shape[1]
+    fetch = pltpu.make_async_copy(lifted_in, lifted, local_sem.at[2])
+    fetch.start()
     bin_count, pix_count = prob_sum.shape
     cols = edges.shape[1]
     rows = sides.shape[1]
@@ -398,6 +413,7 @@
     pix_row = row_iota(pix_count)
     bin_row = row_iota(bin_count)
     clear_border(field, rows, cols)
+    fetch.wait()
 
     def load_row(x, carry):
         field[pl.ds(pl.multiple_of((x + 1) * PITCH + 8, 8), cols), :] = lifted[
@@ -405,7 +421,7 @@
         ].astype(F32)
         return carry
 
-    lax.fori_loop(0, rows, load_row, 0)
+    lax.fori_loop(0, rows, load_row, 0, unroll=4)
     fill_borders(field, edges, sides, rows, cols)
     pl.semaphore_wait(barrier, count - 1)
     first = halo_copies(edges, sides, landed.at[0], halo_send.at[0], halo_recv.at[0])
@@ -438,7 +454,7 @@
         slopes_in[0:code_dims, at] = jnp.concatenate(two, axis=1)
         return carry
 
-    lax.fori_loop(0, rows // 2, take_slopes, 0)
+    lax.fori_loop(0, rows // 2, take_slopes, 0, unroll=4)
     finish_halo(first, landed.at[0], field, rows, cols)
     spread_columns(field, wide, rows, cols)
 
@@ -503,8 +519,8 @@
 
     chips, half = count // 2, owners // 2
     bx, by, _, row_devices = grid_place()
-    core = lax.rem(bx, 2)
-    chip = lax.div(bx, 2) * row_devices + by
+    core = shared(bx, 2)
+    chip = parted(bx, 2) * row_devices + by
     to_sibling = pltpu.make_async_remote_copy(
         src_ref=parts.at[pl.ds((1 - core) * half, half)],
         dst_ref=paired,
@@ -525,13 +541,13 @@
     )
 
     def same_core(one):
-        return (2 * lax.div(one, row_devices) + core, lax.rem(one, row_devices))
+        return (2 * parted(one, row_devices) + core, shared(one, row_devices))
 
     def share_of(one):
-        return lax.rem(one * STRIDE, chips)
+        return shared(one * STRIDE, chips)
 
     def send_part(step, carry):
-        target = lax.rem(chip + step, chips)
+        target = shared(chip + step, chips)
         share = share_of(target)
 
         @pl.when(share < half)
@@ -588,7 +604,7 @@
             def add(sender, total):
                 return total + gathered[sender].astype(F32)
 
-            sums[mine] = lax.fori_loop(0, chips, add, jnp.zeros((SHARE, channels), F32)).astype(
+            sums[mine] = lax.fori_loop(0, chips, add, jnp.zeros((SHARE, channels), F32), unroll=8).astype(
                 BF16
             )
 
@@ -598,7 +614,7 @@
                     dst_ref=sums.at[mine],
                     send_sem=sum_send,
                     recv_sem=sum_recv,
-                    device_id=same_core(lax.rem(chip + step, chips)),
+                    device_id=same_core(shared(chip + step, chips)),
                     device_id_type=MESH,
                 ).start()
                 return carry
@@ -621,7 +637,7 @@
             ]
         return carry
 
-    lax.fori_loop(0, rows // 2, put_codes, 0)
+    lax.fori_loop(0, rows // 2, put_codes, 0, unroll=4)
     for q in range(code_dims):
         codes_out[q] = by_row[pl.ds(q * rows, rows), :].T
 
@@ -638,7 +654,7 @@
         prob_grad, ctx_grad = prob_sum[...], ctx_sum[...]
         for part in range(GROUP):
             turn = group * GROUP + part
-            met = lax.rem(pairs - turn, pairs)
+            met = shared(pairs - turn, pairs)
             code = slot_code[pl.ds(met, 1), :]
             grad = back[pl.ds(2 * turn, 2)].reshape(2 * capacity, channels)
             hot = jnp.right_shift(code, 6) == pix_row
@@ -714,6 +730,7 @@
     run = all_cells // FOLD
     vmem = pl.BlockSpec(memory_space=pltpu.VMEM)
     smem = pl.BlockSpec(memory_space=pltpu.SMEM)
+    anywhere = pl.BlockSpec(memory_space=pl.ANY)
     wide = pltpu.VMEM(((rows + 2) * cols, 3 * channels), BF16)
     blocks = pltpu.VMEM((count, capacity, channels), BF16)
     doubled = pltpu.VMEM((12 * channels, 2 * channels), BF16)
@@ -766,10 +783,11 @@
             jax.ShapeDtypeStruct((pix_count, channels), F32),
             jax.ShapeDtypeStruct((owners, SHARE, channels), BF16),
         ),
-        in_specs=[smem] + [vmem] * 7 + [pl.BlockSpec(memory_space=pl.ANY)],
+        in_specs=[smem, anywhere] + [vmem] * 6 + [anywhere],
         out_specs=(vmem,) * 4,
         scratch_shapes=[
             pltpu.SMEM((capacity, count), I32),
+            pltpu.VMEM((all_cells, channels), BF16),
             blocks,
             blocks,
             pltpu.VMEM(((rows + 2) * PITCH, channels), F32),
@@ -791,7 +809,7 @@
             pltpu.VMEM((8, all_cells), F32),
             pltpu.VMEM((code_dims * rows, cols), F32),
             pltpu.VMEM((8, all_cells), F32),
-            dma((2,)),
+            dma((3,)),
             dma,
             dma((pairs // GROUP,)),
             dma((2, 8)),

time: 116 us -> 113 us (0.974); the launches traced: 116 us -> 111 us
  Pallas kernels: 116 us -> 110 us
    pallas_call x1, Pallas kernels: 67.8 us -> 62.9 us  [per_device(): pl.pallas_call(tile_kernel, out_shape=(jax.ShapeDtypeStruct((code_dims, c...]
where the time goes in v5:
time: 113 us; the launch traced here: 111 us
  Pallas kernels  110 us (97%)
    pallas_call x1, Pallas kernels, per_device(): pl.pallas_call(tile_kernel, out_shape=(jax.ShapeDtypeStruct((code_dims, c...  62.9 us
    pallas_call x1, Pallas kernels, per_device(): pl.pallas_call(lift_kernel, out_shape=(jax.ShapeDtypeStruct((all_cells, c...  45.3 us

profile of v5, /device:TPU:1, one launch (start us, length us, event | category | flops | bytes accessed | tf_op | source)
XLA Modules:
  0.0 111.1 jit_solution(13362599898184708320)
XLA Ops:
  0.6 45.3 %lift.1 = (bf16[8192,128]{1,0:T(8,128)(2,1)}, s32[64,128]{1,0:T(8,128)}, f32[64,128]{1,0:T(8,128)}, f32[64,128]{1,0:T(8,128)}, bf16[128,128]{1,0:T(8,128)(2,1)}) custom-call(s32[1,128]{1,0:T(1,128)} %counts.1, bf16[128,256]{1,0:T(8,128)(2,1)} %features.1, f32[64,128]{1,0:T(8,128)} %logits.1, bf16[256,128]{1,0:T(8,128)(2,1)} %ctx_weight.3, ...), custom_call_target="tpu_custom_call" | custom-call | tf_op jit(solution)/shard_map/lift/pallas_call | solution.py:741
  46.0 62.9 %tile.1 = (f32[6,64,128]{2,1,0:T(8,128)}, f32[64,128]{1,0:T(8,128)}, f32[128,128]{1,0:T(8,128)}, bf16[74,16,128]{2,1,0:T(8,128)(2,1)}) custom-call(s32[6]{0:T(128)} %levels.1, bf16[8192,128]{1,0:T(8,128)(2,1)} %get-tuple-element.19.lifted_in, s32[64,128]{1,0:T(8,128)} %get-tuple-element.20.slot_code, f32[64,128]{1,0:T(8,128)} %get-tuple-element.21.slot_weight, ...), custom_call_target="tpu_custom_call" | custom-call | tf_op jit(solution)/shard_map/tile/pallas_call | solution.py:778
  108.9 2.1 %finish.1 = (f32[6,64,128]{2,1,0:T(8,128)}, f32[64,128]{1,0:T(8,128)}, bf16[128,256]{1,0:T(8,128)(2,1)}, f32[1152,128]{1,0:T(8,128)}, f32[6,128]{1,0:T(8,128)}) custom-call(f32[6,64,128]{2,1,0:T(8,128)} %get-tuple-element.23.codes, f32[64,128]{1,0:T(8,128)} %get-tuple-element.24.prob, f32[64,128]{1,0:T(8,128)} %get-tuple-element.25.prob_grad, ...), custom_call_target="tpu_custom_call" | custom-call | tf_op jit(solution)/shard_map/finish/pallas_call | solution.py:841

commit v6 on v5

--- a/solution.py
+++ b/solution.py
@@ -342,7 +342,7 @@
     own = pltpu.make_async_copy(outgoing.at[my_side], arrived.at[my_side], local_sem)
     own.start()
 
-    cells_v[...] = cells_in[...].T
+    cells_v[0:count] = cells_in[...].T
     cells_two[...] = jnp.concatenate(
         [cells_v[pl.ds(side, pairs, stride=2), :] for side in range(2)], axis=1
     )
@@ -751,7 +751,7 @@
             out_specs=(vmem,) * 5,
             scratch_shapes=[
                 pltpu.VMEM((pairs, 2 * capacity), I32),
-                pltpu.VMEM((count, capacity), I32),
+                pltpu.VMEM((count + 8, capacity), I32),
                 pltpu.SMEM((count,), I32),
                 pltpu.VMEM(pixels.shape, I32),
                 blocks,
@@ -807,7 +807,7 @@
             doubled,
             pltpu.VMEM((16, channels), F32),
             pltpu.VMEM((8, all_cells), F32),
-            pltpu.VMEM((code_dims * rows, cols), F32),
+            pltpu.VMEM(((code_dims + 1) * rows, cols), F32),
             pltpu.VMEM((8, all_cells), F32),
             dma((3,)),
             dma,

time: 113 us -> 113 us (level)
  no operation moved by 1% of the time
where the time goes in v6:
time: 113 us; the launch traced here: 111 us
  Pallas kernels  110 us (97%)
    pallas_call x1, Pallas kernels, per_device(): pl.pallas_call(tile_kernel, out_shape=(jax.ShapeDtypeStruct((code_dims, c...  62.9 us
    pallas_call x1, Pallas kernels, per_device(): pl.pallas_call(lift_kernel, out_shape=(jax.ShapeDtypeStruct((all_cells, c...  45.3 us

profile of v6, /device:TPU:1, one launch (start us, length us, event | category | flops | bytes accessed | tf_op | source)
XLA Modules:
  0.0 111.1 jit_solution(15228163233931489496)
XLA Ops:
  0.6 45.3 %lift.1 = (bf16[8192,128]{1,0:T(8,128)(2,1)}, s32[64,128]{1,0:T(8,128)}, f32[64,128]{1,0:T(8,128)}, f32[64,128]{1,0:T(8,128)}, bf16[128,128]{1,0:T(8,128)(2,1)}) custom-call(s32[1,128]{1,0:T(1,128)} %counts.1, bf16[128,256]{1,0:T(8,128)(2,1)} %features.1, f32[64,128]{1,0:T(8,128)} %logits.1, bf16[256,128]{1,0:T(8,128)(2,1)} %ctx_weight.3, ...), custom_call_target="tpu_custom_call" | custom-call | tf_op jit(solution)/shard_map/lift/pallas_call | solution.py:741
  46.0 62.9 %tile.1 = (f32[6,64,128]{2,1,0:T(8,128)}, f32[64,128]{1,0:T(8,128)}, f32[128,128]{1,0:T(8,128)}, bf16[74,16,128]{2,1,0:T(8,128)(2,1)}) custom-call(s32[6]{0:T(128)} %levels.1, bf16[8192,128]{1,0:T(8,128)(2,1)} %get-tuple-element.19.lifted_in, s32[64,128]{1,0:T(8,128)} %get-tuple-element.20.slot_code, f32[64,128]{1,0:T(8,128)} %get-tuple-element.21.slot_weight, ...), custom_call_target="tpu_custom_call" | custom-call | tf_op jit(solution)/shard_map/tile/pallas_call | solution.py:778
  108.9 2.1 %finish.1 = (f32[6,64,128]{2,1,0:T(8,128)}, f32[64,128]{1,0:T(8,128)}, bf16[128,256]{1,0:T(8,128)(2,1)}, f32[1152,128]{1,0:T(8,128)}, f32[6,128]{1,0:T(8,128)}) custom-call(f32[6,64,128]{2,1,0:T(8,128)} %get-tuple-element.23.codes, f32[64,128]{1,0:T(8,128)} %get-tuple-element.24.prob, f32[64,128]{1,0:T(8,128)} %get-tuple-element.25.prob_grad, ...), custom_call_target="tpu_custom_call" | custom-call | tf_op jit(solution)/shard_map/finish/pallas_call | solution.py:841
